TPU v7x, 512 devices: a whole 4x4x16 slice. The times are simulated.
512 devices in a mesh: scen: 16 (over y, x_lo, core), row: 32 (over z, x_hi).
Axes of the slice: x: 4 (x_hi: 2, x_lo: 2; x = x_hi * 2 + x_lo), y: 4, z: 16, core: 2. Of those that a mesh axis runs over, the one named last changes fastest.
Arguments:
- borders: bfloat16 [16, 1024, 12288], P('scen', None, 'row'), may hold values from -1.078125 to 1.078125
- kkt_inverse: bfloat16 [16, 1024, 1024], P('scen', 'row'), may hold values from -0.35 to 2.35, as said below
- first_section: float32 [12288, 256], P('row'), may hold values from -6 to 6
- barrier: float32 [12288], P('row'), may hold values from 64 to 512
- panel_vars: int32 [256], replicated, may hold values from 0 to 12287, as said below
- probability: float32 [16], replicated, may hold values from 0.5 to 2
- assignment: int32 [16], P('scen'), may hold values from 0 to 15, each once
Outputs:
- factor: float32 [12288, 256], P('row')
Inputs may be any that keep to these rules, and one draw needn't show every extreme that they name: `panel_vars`: distinct values. `kkt_inverse`: each scenario's matrix is symmetric positive definite. `assignment`: each scenario once.
All inputs are finite; a program needn't handle non-finite values.
Results may differ from a plain program's by a relative error of at most 0.00031.
Values may be sent and summed in bfloat16 or wider, within the bound.
No kernel may reach another device: no remote copies, remote signals or barrier semaphores. Data moves between devices by JAX's collectives and lax.ppermute only.
A program may use at most 64 MiB of HBM per device.

v0:
```python
import jax
import jax.numpy as jnp
from jax import lax
from jax.sharding import Mesh
from jax.sharding import PartitionSpec as P

PANEL = 128
PANELS = 2
ROW = ("row_0", "row_1")
SCEN_ROW = ("scen", "row_0", "row_1")


def filled_up(lines, length):
    spare = -len(lines) % length
    return jnp.pad(lines, [(0, spare)] + [(0, 0)] * (lines.ndim - 1))


def own_block_2(blocks, axes, order):
    inside = blocks.shape[1:]
    blocks = blocks.reshape(*(lax.axis_size(a) for a in axes), *inside)
    blocks = jnp.moveaxis(blocks, order, range(len(axes))).reshape(-1, *inside)
    for k in order:
        blocks = lax.psum_scatter(blocks, axes[k], scatter_dimension=0, tiled=True)
    return blocks[0]


def stacked_from(x, axes, order):
    blocks = x[None]
    for k in order:
        blocks = lax.all_gather(blocks, axes[k], axis=0, tiled=True)
    held = [lax.axis_size(axes[k]) for k in reversed(order)]
    blocks = blocks.reshape(*held, *x.shape)
    turned = sorted(range(len(order)), key=lambda place: order[len(order) - 1 - place])
    return blocks.transpose(*turned, *range(len(order), blocks.ndim)).reshape(-1, *x.shape)


def sum_by_parts(x, axes, order):
    length, lines = (lax.axis_size(axes), x.reshape(-1, *x.shape[1:][-1:]))
    blocks = filled_up(lines, length).reshape(length, -1, *lines.shape[1:])
    own = own_block_2(blocks, axes, order)
    whole = stacked_from(own, axes, order[::-1]).reshape(-1, *lines.shape[1:])
    return whole[: len(lines)].reshape(x.shape)


def from_everyone(x, axis):
    copies = jnp.broadcast_to(x, (lax.axis_size(axis), *x.shape))
    return lax.all_to_all(copies, axis, split_axis=0, concat_axis=0, tiled=True)


def in_order(blocks, dim):
    dims = list(blocks.shape[1:])
    dims[dim] *= blocks.shape[0]
    return jnp.moveaxis(blocks, 0, dim).reshape(dims)


def collect(x, axis, dim):
    blocks = from_everyone(x, axis)
    return in_order(blocks, dim)


def split_up(x, dim, length):
    dims = x.shape
    blocks = x.reshape(*dims[:dim], length, dims[dim] // length, *dims[dim + 1 :])
    return jnp.moveaxis(blocks, dim, 0)


def summed_on_arrival(x, axis, dim):
    length = lax.axis_size(axis)
    blocks = lax.all_to_all(split_up(x, dim, length), axis, 0, 0, tiled=True)
    return jnp.sum(blocks, axis=0)


def factorize(diag_block, row_block):
    symmetric = 0.5 * (diag_block + diag_block.T)
    block_parts = []
    row_parts = []
    for panel_index in range(PANELS):
        low_col = panel_index * PANEL
        high_col = low_col + PANEL
        block_cols = symmetric[:, low_col:high_col]
        row_cols = row_block[:, low_col:high_col]
        if panel_index > 0:
            earlier_block = block_parts[0]
            earlier_rows = row_parts[0]
            across = earlier_block[low_col:high_col, :]
            block_cols = block_cols - jnp.dot(
                earlier_block, across.T, precision=lax.Precision.HIGHEST
            )
            row_cols = row_cols - jnp.dot(earlier_rows, across.T, precision=lax.Precision.HIGHEST)
        panel_chol = jnp.linalg.cholesky(block_cols[low_col:high_col, :])
        block_parts.append(
            lax.linalg.triangular_solve(
                panel_chol, block_cols, left_side=False, lower=True, transpose_a=True
            )
        )
        row_parts.append(
            lax.linalg.triangular_solve(
                panel_chol, row_cols, left_side=False, lower=True, transpose_a=True
            )
        )
    return jnp.concatenate(row_parts, axis=1)


def per_device(borders, kkt_inverse, first_section, barrier, panel_vars, probability, assignment):
    rows_dev = first_section.shape[0]
    first_row = lax.axis_index(ROW) * rows_dev
    local_index = panel_vars - first_row
    inside = (local_index >= 0) & (local_index < rows_dev)
    clipped = jnp.clip(local_index, 0, rows_dev - 1)
    picked = jnp.take(borders, clipped, axis=2) * inside.astype(jnp.bfloat16)[None, None, :]
    columns = sum_by_parts(picked, ROW, (0, 1)).astype(jnp.float32).astype(jnp.bfloat16)
    own_solved = jnp.einsum(
        "sij,sjc->sic", kkt_inverse, columns, preferred_element_type=jnp.float32
    ).astype(jnp.bfloat16)
    solved = collect(own_solved, ROW, 1)
    scen_count = probability.shape[0]
    matches = assignment[:, None] == jnp.arange(scen_count, dtype=jnp.int32)[None, :]
    weight = jnp.sum(jnp.where(matches, probability[None, :], 0.0), axis=1)
    leading = (lax.axis_index("scen") == 0).astype(jnp.float32)
    hits = jnp.arange(rows_dev, dtype=jnp.int32)[:, None] + first_row == panel_vars[None, :]
    baseline = first_section + jnp.where(hits, barrier[:, None], 0.0)
    term = jnp.einsum("snr,snc->src", borders, solved, preferred_element_type=jnp.float32)
    contribution = jnp.sum(term * weight[:, None, None], axis=0) + leading * baseline
    own_block = jnp.take(contribution, clipped, axis=0) * inside.astype(jnp.float32)[:, None]
    diag_block = lax.psum(own_block, SCEN_ROW)
    shares = summed_on_arrival(contribution, "scen", 0)
    factor_part = factorize(diag_block, shares)
    factor = collect(factor_part, "scen", 0)
    return factor


def solution(mesh):
    torus = Mesh(mesh.devices.reshape(mesh.shape["scen"], 16, 2), ("scen", "row_0", "row_1"))
    return jax.shard_map(
        per_device,
        mesh=torus,
        in_specs=(
            P("scen", None, ROW),
            P("scen", ROW, None),
            P(ROW, None),
            P(ROW),
            P(),
            P(),
            P("scen"),
        ),
        out_specs=P(ROW, None),
        check_vma=False,
    )
```

profile of v0, /device:TPU:1, one launch (start us, length us, event | category | flops | bytes accessed | tf_op | source)
XLA Modules:
  0.0 706.2 jit_solution(5886674217138400960)
XLA Ops:
  7.3 1.4 copy.24
  8.7 1.2 gather_fusion
  10.1 0.8 select_multiply_fusion
  11.0 63.3 %reduce-scatter.3.cloned.1.call-done = bf16[2,32,256]{2,1,0:T(8,128)(2,1)} async-done(((bf16[32,32,256]{2,1,0:T(8,128)(2,1)}), bf16[2,32,256]{2,1,0:T(8,128)(2,1)}) %reduce-scatter.3.cloned.1.call-update) | async-done | bytes 32784 | tf_op jit(solution)/shard_map/reduce_scatter | solution.py:23
  74.4 33.0 %reduce-scatter.5.cloned.1.call-done = bf16[1,32,256]{2,1,0:T(8,128)(2,1)} async-done(((bf16[2,32,256]{2,1,0:T(8,128)(2,1)}), bf16[1,32,256]{2,1,0:T(8,128)(2,1)}) %reduce-scatter.5.cloned.1.call-update) | async-done | bytes 16400 | tf_op jit(solution)/shard_map/reduce_scatter | solution.py:23
  107.4 5.0 all_gather.6
  112.3 26.8 %all_gather.7 = bf16[32,32,256]{2,1,0:T(8,128)(2,1)S(1)} all-gather(bf16[2,32,256]{2,1,0:T(8,128)(2,1)S(1)} %all_gather.6), channel_id=1, replica_groups=mesh['scen'=16,'row_0'=16,'row_1'=2] {'row_0'}, dimensions={0}, use_global_device_ids=true | all-gather | bytes 557056 | tf_op jit(solution)/shard_map/all_gather | solution.py:30
  139.3 0.8 broadcast_in_dim.58
  140.2 8.6 %all-to-all-start = ((bf16[32,1,32,256]{3,2,1,0:T(8,128)(2,1)}), bf16[32,1,32,256]{3,2,1,0:T(8,128)(2,1)S(1)}, u32[]{:S(2)}, u32[]{:S(2)}) async-start(bf16[32,1,32,256]{3,2,1,0:T(8,128)(2,1)} %broadcast_in_dim.58), calls=%async_computation.2 | async-start | bytes 1048576 | tf_op jit(solution)/shard_map/all_to_all | solution.py:47
  151.0 21.0 %all-to-all-done = bf16[32,1,32,256]{3,2,1,0:T(8,128)(2,1)S(1)} async-done(((bf16[32,1,32,256]{3,2,1,0:T(8,128)(2,1)}), bf16[32,1,32,256]{3,2,1,0:T(8,128)(2,1)S(1)}, u32[]{:S(2)}, u32[]{:S(2)}) %all-to-all-start) | async-done | bytes 524320 | tf_op jit(solution)/shard_map/all_to_all | solution.py:47
  172.0 1.2 fusion.1
  173.2 0.9 copy.27
  174.1 2.0 gather_fusion.1
  176.1 0.8 select_multiply_fusion.1
  177.0 15.9 %all-to-all-start.1 = ((f32[16,24,256]{2,1,0:T(8,128)}), f32[16,24,256]{2,1,0:T(8,128)S(1)}, u32[]{:S(2)}, u32[]{:S(2)}) async-start(f32[16,24,256]{2,1,0:T(8,128)} %bitcast.13), calls=%async_computation.3 | async-start | bytes 786432 | tf_op jit(solution)/shard_map/all_to_all | solution.py:69
  192.9 441.5 %all-reduce.2.cloned.1.call-done = f32[256,256]{1,0:T(8,128)} async-done(((f32[256,256]{1,0:T(8,128)}), f32[256,256]{1,0:T(8,128)}) %all-reduce.2.cloned.1.call-update) | async-done | bytes 262160 | tf_op jit(solution)/shard_map/psum | solution.py:125
  634.3 1.1 copy.28
  635.7 11.7 %cholesky.44 = f32[128,128]{1,0:T(8,128)S(1)} custom-call(f32[128,128]{1,0:T(8,128)S(1)} %fusion.13), custom_call_target="Cholesky" | custom-call | tf_op jit(solution)/shard_map/jit(cholesky)/cholesky | solution.py:90
  648.8 9.8 %custom-call.10 = f32[1,128,128]{1,2,0:T(8,128)S(1)} custom-call(f32[1,128,128]{2,1,0:T(8,128)S(1)} %fusion.7), custom_call_target="InvertDiagBlocksLowerTriangular" | custom-call | tf_op jit(solution)/shard_map/triangular_solve/custom-call.0 | solution.py:97
  660.0 11.7 %cholesky.55 = f32[128,128]{1,0:T(8,128)S(1)} custom-call(f32[128,128]{1,0:T(8,128)S(1)} %fusion.10), custom_call_target="Cholesky" | custom-call | tf_op jit(solution)/shard_map/jit(cholesky)/cholesky | solution.py:90
  671.8 0.7 compare_reduce_fusion
  673.2 9.8 %custom-call.11 = f32[1,128,128]{1,2,0:T(8,128)S(1)} custom-call(f32[1,128,128]{2,1,0:T(8,128)S(1)} %fusion.8), custom_call_target="InvertDiagBlocksLowerTriangular" | custom-call | tf_op jit(solution)/shard_map/triangular_solve/custom-call.0 | solution.py:97
  683.7 15.3 %all_to_all.15 = f32[16,24,256]{2,1,0:T(8,128)S(1)} all-to-all(f32[16,24,256]{2,1,0:T(8,128)S(1)} %broadcast_in_dim.63), channel_id=1, replica_groups=mesh['scen'=16,'row_0'=16,'row_1'=2] {'scen'}, dimensions={0} | all-to-all | bytes 786432 | tf_op jit(solution)/shard_map/all_to_all | solution.py:47
  699.0 0.7 copy.37
  (53 shorter events, 7.0 us)
Async XLA Ops:
  6.5 132.6 %copy-start = (bf16[1,32,1024]{2,1,0:T(8,128)(2,1)S(1)}, bf16[1,32,1024]{2,1,0:T(8,128)(2,1)}, u32[]{:S(2)}) copy-start(bf16[1,32,1024]{2,1,0:T(8,128)(2,1)} %param.11) | copy-start | bytes 196612
  6.5 67.8 %reduce-scatter.3.cloned.1.call-start = ((), (), s32[]{:S(2)}) async-start(), calls=%async_computation.5 | async-start | bytes 557056 | tf_op jit(solution)/shard_map/reduce_scatter | solution.py:23
  6.5 0.7 copy-start.5
  10.9 96.4 %reduce-scatter.5.cloned.1.call-start = ((), (), s32[]{:S(2)}) async-start(), calls=%async_computation.6 | async-start | bytes 49152 | tf_op jit(solution)/shard_map/reduce_scatter | solution.py:23
  139.3 9.5 %copy-start.4 = (f32[384,256]{1,0:T(8,128)S(1)}, f32[384,256]{1,0:T(8,128)}, u32[]{:S(2)}) copy-start(f32[384,256]{1,0:T(8,128)} %param.12) | copy-start | bytes 1179652
  140.2 31.8 %copy-start.3 = (bf16[1,1024,384]{2,1,0:T(8,128)(2,1)S(1)}, bf16[1,1024,384]{2,1,0:T(8,128)(2,1)}, u32[]{:S(2)}) copy-start(bf16[1,1024,384]{2,1,0:T(8,128)(2,1)} %param.10) | copy-start | bytes 2359300
  140.2 31.8 %all-to-all-start = ((bf16[32,1,32,256]{3,2,1,0:T(8,128)(2,1)}), bf16[32,1,32,256]{3,2,1,0:T(8,128)(2,1)S(1)}, u32[]{:S(2)}, u32[]{:S(2)}) async-start(bf16[32,1,32,256]{3,2,1,0:T(8,128)(2,1)} %broadcast_in_dim.58), calls=%async_computation.2 | async-start | bytes 1048576 | tf_op jit(solution)/shard_map/all_to_all | solution.py:47
  148.8 485.5 %all-reduce.2.cloned.1.call-start = ((), (), s32[]{:S(2)}) async-start(), calls=%async_computation.7 | async-start | bytes 524288 | tf_op jit(solution)/shard_map/psum | solution.py:125
  149.7 0.7 copy-start.7
  150.4 21.7 %copy-start.6 = (f32[384]{0:T(512)S(1)}, f32[384]{0:T(512)}, u32[]{:S(2)}) copy-start(f32[384]{0:T(512)} %param.13) | copy-start | bytes 4612
  177.0 506.1 %all-to-all-start.1 = ((f32[16,24,256]{2,1,0:T(8,128)}), f32[16,24,256]{2,1,0:T(8,128)S(1)}, u32[]{:S(2)}, u32[]{:S(2)}) async-start(f32[16,24,256]{2,1,0:T(8,128)} %bitcast.13), calls=%async_computation.3 | async-start | bytes 786432 | tf_op jit(solution)/shard_map/all_to_all | solution.py:69
  634.3 1.2 copy-start.2
  635.5 23.0 %copy-start.1 = (f32[256,256]{0,1:T(8,128)}, f32[256,256]{0,1:T(8,128)S(1)}, u32[]{:S(2)}) copy-start(f32[256,256]{0,1:T(8,128)S(1)} %fusion.4) | copy-start | bytes 786436
  659.0 0.9 slice-start
Sparse Core Ops, SparseCore 0:
  11.1 63.2 reduce-scatter.2
  77.3 30.0 reduce-scatter.4
  177.1 457.2 all-reduce.1
where the time goes:
time: 707 us; the launch traced here: 706 us
  waiting for transfers between devices  559 us (79%)
  other arithmetic  48.4 us (7%)
  blocking collectives  47 us (7%)
  starting transfers between devices  24.6 us (3%)
  between operations  14.1 us (2%)
  local copies, waits for them, and re-layouts  10.8 us (2%)
    psum x1, waiting for transfers between devices, per_device(): diag_block = lax.psum(own_block, SCEN_ROW)  441 us
    reduce_scatter x2, waiting for transfers between devices, own_block_2(): blocks = lax.psum_scatter(blocks, axes[k], scatter_dimension=0, tiled=True)  96.3 us
    all_gather x2, blocking collectives, stacked_from(): blocks = lax.all_gather(blocks, axes[k], axis=0, tiled=True)  31.8 us
    another operation x6, other arithmetic, factorize(): panel_chol = jnp.linalg.cholesky(block_cols[low_col:high_col, :])  24.9 us
    all_to_all x1, waiting for transfers between devices, from_everyone(): return lax.all_to_all(copies, axis, split_axis=0, concat_axis=0, tiled=True)  21 us
    another operation x4, other arithmetic, factorize(): lax.linalg.triangular_solve(panel_chol, row_cols, left_side=False, lower=...  20.9 us
    all_to_all x1, starting transfers between devices, summed_on_arrival(): blocks = lax.all_to_all(split_up(x, dim, length), axis, 0, 0, tiled=True)  15.9 us
    all_to_all x1, blocking collectives, from_everyone(): return lax.all_to_all(copies, axis, split_axis=0, concat_axis=0, tiled=True)  15.3 us
  transfers between devices with their start and end apart: 5, of which 4 were waited for; matrix products, arithmetic and copies ran while one was open for 7% of the time, Pallas kernels for 0%

commit v1 on v0

v1 whole, which is shorter than its diff:
```python
import jax
import jax.numpy as jnp
from jax import lax
from jax.sharding import Mesh
from jax.sharding import PartitionSpec as P

PANEL = 128
PANELS = 2
SLOTS = 24
ROW = ("z", "xh")
HIGHEST = lax.Precision.HIGHEST


def split_in_three(x):
    high = x.astype(jnp.bfloat16)
    rest = x - high.astype(jnp.float32)
    middle = rest.astype(jnp.bfloat16)
    low = (rest - middle.astype(jnp.float32)).astype(jnp.bfloat16)
    return high, middle, low


def from_everyone(x, axis):
    copies = jnp.broadcast_to(x, (lax.axis_size(axis), *x.shape))
    return lax.all_to_all(copies, axis, split_axis=0, concat_axis=0, tiled=True)


def swapped(x):
    return lax.ppermute(x, "xh", [(0, 1), (1, 0)])


def factorize(diag_block, row_block):
    symmetric = 0.5 * (diag_block + diag_block.T)
    block_parts = []
    row_parts = []
    for panel_index in range(PANELS):
        low_col = panel_index * PANEL
        high_col = low_col + PANEL
        block_cols = symmetric[:, low_col:high_col]
        row_cols = row_block[:, low_col:high_col]
        if panel_index > 0:
            earlier_block = block_parts[0]
            earlier_rows = row_parts[0]
            across = earlier_block[low_col:high_col, :]
            block_cols = block_cols - jnp.dot(earlier_block, across.T, precision=HIGHEST)
            row_cols = row_cols - jnp.dot(earlier_rows, across.T, precision=HIGHEST)
        panel_chol = jnp.linalg.cholesky(block_cols[low_col:high_col, :])
        block_parts.append(
            lax.linalg.triangular_solve(
                panel_chol, block_cols, left_side=False, lower=True, transpose_a=True
            )
        )
        row_parts.append(
            lax.linalg.triangular_solve(
                panel_chol, row_cols, left_side=False, lower=True, transpose_a=True
            )
        )
    return jnp.concatenate(row_parts, axis=1)


def per_device(borders, kkt_inverse, first_section, barrier, panel_vars, probability, assignment):
    border, inverse_rows = borders[0], kkt_inverse[0]
    rows_dev, win = first_section.shape
    z_count, scen_count = lax.axis_size("z"), lax.axis_size("scen")
    rows_inv = inverse_rows.shape[0]
    me_xh = lax.axis_index("xh")
    me_row = lax.axis_index("z") * 2 + me_xh
    me_scen = lax.axis_index("scen")

    other_rows = swapped(inverse_rows)
    first_half = jnp.where(me_xh == 0, inverse_rows, other_rows)
    second_half = jnp.where(me_xh == 0, other_rows, inverse_rows)
    inverse_pair = jnp.concatenate([first_half, second_half], axis=0)

    owner = panel_vars // rows_dev
    local = panel_vars - owner * rows_dev
    same = (owner[:, None] == owner[None, :]) & (jnp.arange(win)[:, None] > jnp.arange(win)[None, :])
    rank = jnp.sum(same.astype(jnp.int32), axis=1)
    rounds = jnp.max(rank) // SLOTS + 1

    def gather_round(turn):
        place = rank - turn * SLOTS
        slot = jnp.arange(SLOTS, dtype=jnp.int32)
        mine = (owner[None, :] == me_row) & (place[None, :] == slot[:, None])
        source = jnp.sum(jnp.where(mine, local[None, :] + 1, 0), axis=1) - 1
        pick = (source[:, None] == jnp.arange(rows_dev)[None, :]).astype(jnp.bfloat16)
        picked = lax.dot_general(
            pick, border, (((1,), (1,)), ((), ())), preferred_element_type=jnp.float32
        ).astype(jnp.bfloat16)
        everyone = lax.all_gather(picked, "z", axis=0, tiled=True)
        holder = jnp.arange(z_count * SLOTS, dtype=jnp.int32)
        put = (owner[None, :] == (holder // SLOTS * 2 + me_xh)[:, None]) & (
            place[None, :] == (holder % SLOTS)[:, None]
        )
        return lax.dot_general(
            everyone,
            put.astype(jnp.bfloat16),
            (((0,), (0,)), ((), ())),
            preferred_element_type=jnp.float32,
        ).astype(jnp.bfloat16)

    half_columns = gather_round(jnp.int32(0))
    _, half_columns = lax.while_loop(
        lambda state: state[0] < rounds,
        lambda state: (state[0] + 1, state[1] + gather_round(state[0])),
        (jnp.int32(1), half_columns),
    )
    columns = half_columns + swapped(half_columns)

    share = win // scen_count
    share_vars = lax.dynamic_slice(panel_vars, (me_scen * share,), (share,)) - me_row * rows_dev
    held = (share_vars >= 0) & (share_vars < rows_dev)
    at = jnp.clip(share_vars, 0, rows_dev - 1)
    window_place = me_scen * share + jnp.arange(share, dtype=jnp.int32)
    on_diagonal = window_place[:, None] == jnp.arange(win, dtype=jnp.int32)[None, :]
    base = jnp.take(first_section, at, axis=0) + jnp.where(
        on_diagonal, jnp.take(barrier, at)[:, None], 0.0
    )
    base = jnp.where(held[:, None], base, 0.0)

    own_solved = jnp.dot(inverse_pair, half_columns, preferred_element_type=jnp.float32)
    message = jnp.concatenate([own_solved.astype(jnp.bfloat16), *split_in_three(base)], axis=0)
    both = lax.all_gather(message, "xh", axis=0)
    message = both[0] + both[1]
    gathered = lax.all_gather(message, "z", axis=0)
    solved = gathered[:, : 2 * rows_inv].reshape(-1, win)
    parts = jnp.sum(gathered[:, 2 * rows_inv :].astype(jnp.float32), axis=0)
    base_share = parts[:share] + parts[share : 2 * share] + parts[2 * share :]

    matches = assignment[:, None] == jnp.arange(scen_count, dtype=jnp.int32)[None, :]
    weight = jnp.sum(jnp.where(matches, probability[None, :], 0.0))

    block_term = weight * lax.dot_general(
        columns, solved, (((0,), (0,)), ((), ())), preferred_element_type=jnp.float32
    )
    block_shares = lax.all_to_all(
        block_term.reshape(scen_count, share, win), "scen", 0, 0, tiled=True
    )
    block_share = jnp.sum(block_shares, axis=0) + base_share
    diag_block = from_everyone(block_share, "scen").reshape(win, win)

    term = weight * lax.dot_general(
        border, solved, (((0,), (0,)), ((), ())), preferred_element_type=jnp.float32
    )
    term_shares = lax.all_to_all(
        term.reshape(scen_count, rows_dev // scen_count, win), "scen", 0, 0, tiled=True
    )
    term_share = jnp.sum(term_shares, axis=0)
    total = from_everyone(term_share, "scen").reshape(rows_dev, win)
    hits = (
        jnp.arange(rows_dev, dtype=jnp.int32)[:, None] + me_row * rows_dev == panel_vars[None, :]
    )
    rows = total + first_section + jnp.where(hits, barrier[:, None], 0.0)
    return factorize(diag_block, rows)


def solution(mesh):
    torus = Mesh(mesh.devices.reshape(mesh.shape["scen"], 16, 2), ("scen", "z", "xh"))
    return jax.shard_map(
        per_device,
        mesh=torus,
        in_specs=(
            P("scen", None, ROW),
            P("scen", ROW, None),
            P(ROW, None),
            P(ROW),
            P(),
            P(),
            P("scen"),
        ),
        out_specs=P(ROW, None),
        check_vma=False,
    )
```

time: 707 us -> 202 us (0.29)
  waiting for transfers between devices: 559 us -> 28.2 us
  blocking collectives: 47 us -> 64.2 us
  starting transfers between devices: 24.6 us -> 41.7 us
  between operations: 14.1 us -> 3.09 us
    psum x1 -> x0, waiting for transfers between devices: 441 us -> none  [per_device(): diag_block = lax.psum(own_block, SCEN_ROW)]
    reduce_scatter x2 -> x0, waiting for transfers between devices: 96.3 us -> none  [own_block_2(): blocks = lax.psum_scatter(blocks, axes[k], scatter_dimension=0, tiled=True)]
    all_gather x2 -> x3, blocking collectives: 31.8 us -> 64.2 us  [the longest x1 33.2 us: gather_round(): everyone = lax.all_gather(picked, 'z', axis=0, tiled=True)]
    all_to_all x1 -> x0, blocking collectives: 15.3 us -> none  [from_everyone(): return lax.all_to_all(copies, axis, split_axis=0, concat_axis=0, tiled=True)]
    all_to_all x1 -> x2, waiting for transfers between devices: 0.01 us -> 12.8 us  [the longest x1 7.2 us: per_device(): lax.all_to_all(block_term.reshape(scen_count, share, win), 'scen', 0, 0,...]
    all_to_all x1 -> x2, starting transfers between devices: 15.9 us -> 25.1 us  [the longest x1 20.6 us: per_device(): lax.all_to_all(term.reshape(scen_count, rows_dev // scen_count, win), 'sc...]
    ppermute x0 -> x2, starting transfers between devices: none -> 7.73 us  [swapped(): return lax.ppermute(x, 'xh', [(0, 1), (1, 0)])]
    all_to_all x1 -> x2, waiting for transfers between devices: 21 us -> 15.4 us  [from_everyone(): return lax.all_to_all(copies, axis, split_axis=0, concat_axis=0, tiled=True)]
  transfers between devices with their start and end apart: 5 -> 6, of which waited for: 4 -> 4; matrix products, arithmetic and copies ran while one was open for 7% -> 5% of each run, Pallas kernels for 0% -> 0%
where the time goes in v1:
time: 202 us; the launch traced here: 201 us
  blocking collectives  64.2 us (32%)
  other arithmetic  48.2 us (24%)
  starting transfers between devices  41.7 us (21%)
  waiting for transfers between devices  28.2 us (14%)
  local copies, waits for them, and re-layouts  8.09 us (4%)
  matrix products  8.06 us (4%)
  between operations  3.09 us (2%)
    all_gather x1, blocking collectives, gather_round(): everyone = lax.all_gather(picked, 'z', axis=0, tiled=True)  33.2 us
    all_gather x1, blocking collectives, per_device(): gathered = lax.all_gather(message, 'z', axis=0)  25.5 us
    another operation x6, other arithmetic, factorize(): panel_chol = jnp.linalg.cholesky(block_cols[low_col:high_col, :])  24.9 us
    another operation x4, other arithmetic, factorize(): lax.linalg.triangular_solve(panel_chol, row_cols, left_side=False, lower=...  21 us
    all_to_all x1, starting transfers between devices, per_device(): lax.all_to_all(term.reshape(scen_count, rows_dev // scen_count, win), 'sc...  20.6 us
    all_to_all x2, waiting for transfers between devices, from_everyone(): return lax.all_to_all(copies, axis, split_axis=0, concat_axis=0, tiled=True)  15.4 us
    all_to_all x2, starting transfers between devices, from_everyone(): return lax.all_to_all(copies, axis, split_axis=0, concat_axis=0, tiled=True)  8.83 us
    ppermute x2, starting transfers between devices, swapped(): return lax.ppermute(x, 'xh', [(0, 1), (1, 0)])  7.73 us
  transfers between devices with their start and end apart: 6, of which 4 were waited for; matrix products, arithmetic and copies ran while one was open for 5% of the time, Pallas kernels for 0%

profile of v1, /device:TPU:1, one launch (start us, length us, event | category | flops | bytes accessed | tf_op | source)
XLA Modules:
  0.0 201.5 jit_solution(10401444490419717712)
XLA Ops:
  0.0 5.5 %collective-permute-start.1 = (bf16[32,1024]{1,0:T(8,128)(2,1)}, bf16[32,1024]{1,0:T(8,128)(2,1)S(1)}, u32[]{:S(2)}, u32[]{:S(2)}) collective-permute-start(bf16[32,1024]{1,0:T(8,128)(2,1)} %bitcast.72), channel_id=1, source_target_pairs={{0,1},{1,0},{2,3},{3,2},{4,5},{5,4},{6,7},{7,6},{8,9},{9,8},{10,11... | collective-permute-start | bytes 196616 | tf_op jit(solution)/shard_map/ppermute | solution.py:28
  9.3 1.4 convolution_convert_fusion.3
  10.8 33.2 %all_gather.20 = bf16[384,1024]{1,0:T(8,128)(2,1)S(1)} all-gather(bf16[24,1024]{1,0:T(8,128)(2,1)S(1)} %convolution_convert_fusion.3), channel_id=1, replica_groups=mesh['scen'=16,'z'=16,'xh'=2] {'z'}, dimensions={0}, use_global_device_ids=true | all-gather | bytes 835584 | tf_op jit(solution)/shard_map/all_gather | solution.py:89
  45.1 2.3 %collective-permute-start = (bf16[1024,256]{1,0:T(8,128)(2,1)S(1)}, bf16[1024,256]{1,0:T(8,128)(2,1)}, u32[]{:S(2)}, u32[]{:S(2)}) collective-permute-start(bf16[1024,256]{1,0:T(8,128)(2,1)S(1)} %get-tuple-element.157), channel_id=1, source_target_pairs={{0,1},{1,0},{2,3},{3,2},{4,5},{5,4},{6,7},{7,6},{8,9},{9,8},{10,11... | collective-permute-start | bytes 1572872 | tf_op jit(solution)/shard_map/ppermute | solution.py:28
  51.7 5.5 %all-gather = bf16[224,256]{1,0:T(8,128)(2,1)S(1)} all-gather(bf16[112,256]{1,0:T(8,128)(2,1)S(1)} %pad_maximum_fusion.1), channel_id=2, replica_groups=mesh['scen'=16,'z'=16,'xh'=2] {'xh'}, dimensions={0}, use_global_device_ids=true | all-gather | bytes 172032 | tf_op jit(solution)/shard_map/all_gather | solution.py:122
  57.3 25.5 %all-gather.1 = bf16[1792,256]{1,0:T(8,128)(2,1)S(1)} all-gather(bf16[112,256]{1,0:T(8,128)(2,1)S(1)} %slice_add_fusion), channel_id=3, replica_groups=mesh['scen'=16,'z'=16,'xh'=2] {'z'}, dimensions={0}, use_global_device_ids=true | all-gather | bytes 974848 | tf_op jit(solution)/shard_map/all_gather | solution.py:124
  82.8 1.1 fusion.19
  83.9 0.9 copy.21
  84.8 20.6 %all-to-all-start.2 = ((f32[16,24,256]{2,1,0:T(8,128)}), f32[16,24,256]{2,1,0:T(8,128)S(1)}, u32[]{:S(2)}, u32[]{:S(2)}) async-start(f32[16,24,256]{2,1,0:T(8,128)} %bitcast.12), calls=%async_computation.2 | async-start | bytes 786432 | tf_op jit(solution)/shard_map/all_to_all | solution.py:144
  105.5 2.8 %convolution_multiply_fusion.1 = f32[256,256]{1,0:T(8,128)} fusion(bf16[1024,256]{1,0:T(8,128)(2,1)S(1)} %bitcast.71, bf16[1024,256]{1,0:T(8,128)(2,1)S(1)} %get-tuple-element.157, bf16[1024,256]{1,0:T(8,128)(2,1)} %collective-permute-done, f32[]{:T(128)} %fusion.60), kind=kOutput, calls=%fused_computation.37 | convolution fusion | flops 134545408 | bytes 1835012 | tf_op jit(solution)/shard_map/dot_general | solution.py:132
  108.2 5.6 %all-to-all-done.2 = f32[16,24,256]{2,1,0:T(8,128)S(1)} async-done(((f32[16,24,256]{2,1,0:T(8,128)}), f32[16,24,256]{2,1,0:T(8,128)S(1)}, u32[]{:S(2)}, u32[]{:S(2)}) %all-to-all-start.2) | async-done | bytes 393248 | tf_op jit(solution)/shard_map/all_to_all | solution.py:144
  113.9 4.5 %all-to-all-start = ((f32[16,16,256]{2,1,0:T(8,128)}), f32[16,16,256]{2,1,0:T(8,128)S(1)}, u32[]{:S(2)}, u32[]{:S(2)}) async-start(f32[16,16,256]{2,1,0:T(8,128)} %bitcast.5), calls=%async_computation | async-start | bytes 524288 | tf_op jit(solution)/shard_map/all_to_all | solution.py:135
  118.4 7.2 %all-to-all-done = f32[16,16,256]{2,1,0:T(8,128)S(1)} async-done(((f32[16,16,256]{2,1,0:T(8,128)}), f32[16,16,256]{2,1,0:T(8,128)S(1)}, u32[]{:S(2)}, u32[]{:S(2)}) %all-to-all-start) | async-done | bytes 262176 | tf_op jit(solution)/shard_map/all_to_all | solution.py:135
  125.6 0.8 broadcast_in_dim.136
  126.3 4.3 %all-to-all-start.3 = ((f32[16,24,256]{2,1,0:T(8,128)}), f32[16,24,256]{2,1,0:T(8,128)S(1)}, u32[]{:S(2)}, u32[]{:S(2)}) async-start(f32[16,24,256]{2,1,0:T(8,128)} %broadcast_in_dim.136), calls=%async_computation.3 | async-start | bytes 786432 | tf_op jit(solution)/shard_map/all_to_all | solution.py:24
  130.8 8.4 %all-to-all-done.3 = f32[16,24,256]{2,1,0:T(8,128)S(1)} async-done(((f32[16,24,256]{2,1,0:T(8,128)}), f32[16,24,256]{2,1,0:T(8,128)S(1)}, u32[]{:S(2)}, u32[]{:S(2)}) %all-to-all-start.3) | async-done | bytes 393248 | tf_op jit(solution)/shard_map/all_to_all | solution.py:24
  139.2 0.7 broadcast_in_dim.135
  139.9 4.5 %all-to-all-start.1 = ((f32[16,16,256]{2,1,0:T(8,128)}), f32[16,16,256]{2,1,0:T(8,128)S(1)}, u32[]{:S(2)}, u32[]{:S(2)}) async-start(f32[16,16,256]{2,1,0:T(8,128)} %broadcast_in_dim.135), calls=%async_computation.1 | async-start | bytes 524288 | tf_op jit(solution)/shard_map/all_to_all | solution.py:24
  144.5 7.1 %all-to-all-done.1 = f32[16,16,256]{2,1,0:T(8,128)S(1)} async-done(((f32[16,16,256]{2,1,0:T(8,128)}), f32[16,16,256]{2,1,0:T(8,128)S(1)}, u32[]{:S(2)}, u32[]{:S(2)}) %all-to-all-start.1) | async-done | bytes 262176 | tf_op jit(solution)/shard_map/all_to_all | solution.py:24
  151.9 11.7 %cholesky.44 = f32[128,128]{1,0:T(8,128)S(1)} custom-call(f32[128,128]{1,0:T(8,128)S(1)} %fusion.43), custom_call_target="Cholesky" | custom-call | tf_op jit(solution)/shard_map/jit(cholesky)/cholesky | solution.py:46
  165.1 9.8 %custom-call.10 = f32[1,128,128]{1,2,0:T(8,128)S(1)} custom-call(f32[1,128,128]{2,1,0:T(8,128)S(1)} %fusion.37), custom_call_target="InvertDiagBlocksLowerTriangular" | custom-call | tf_op jit(solution)/shard_map/triangular_solve/custom-call.0 | solution.py:53
  176.4 11.7 %cholesky.55 = f32[128,128]{1,0:T(8,128)S(1)} custom-call(f32[128,128]{1,0:T(8,128)S(1)} %fusion.40), custom_call_target="Cholesky" | custom-call | tf_op jit(solution)/shard_map/jit(cholesky)/cholesky | solution.py:46
  189.4 9.8 %custom-call.11 = f32[1,128,128]{1,2,0:T(8,128)S(1)} custom-call(f32[1,128,128]{2,1,0:T(8,128)S(1)} %fusion.38), custom_call_target="InvertDiagBlocksLowerTriangular" | custom-call | tf_op jit(solution)/shard_map/triangular_solve/custom-call.0 | solution.py:53
  200.6 0.9 copy.24
  (67 shorter events, 12.6 us)
Async XLA Ops:
  0.0 51.5 %collective-permute-start.1 = (bf16[32,1024]{1,0:T(8,128)(2,1)}, bf16[32,1024]{1,0:T(8,128)(2,1)S(1)}, u32[]{:S(2)}, u32[]{:S(2)}) collective-permute-start(bf16[32,1024]{1,0:T(8,128)(2,1)} %bitcast.72), channel_id=1, source_target_pairs={{0,1},{1,0},{2,3},{3,2},{4,5},{5,4},{6,7},{7,6},{8,9},{9,8},{10,11... | collective-permute-start | bytes 196616 | tf_op jit(solution)/shard_map/ppermute | solution.py:28
  5.5 0.7 copy-start.5
  43.9 1.1 copy-start.1
  45.1 4.4 %copy-start.3 = (f32[384,256]{1,0:T(8,128)S(1)}, f32[384,256]{1,0:T(8,128)}, u32[]{:S(2)}) copy-start(f32[384,256]{1,0:T(8,128)} %param.14) | copy-start | bytes 1179652
  45.1 60.4 %collective-permute-start = (bf16[1024,256]{1,0:T(8,128)(2,1)S(1)}, bf16[1024,256]{1,0:T(8,128)(2,1)}, u32[]{:S(2)}, u32[]{:S(2)}) collective-permute-start(bf16[1024,256]{1,0:T(8,128)(2,1)S(1)} %get-tuple-element.157), channel_id=1, source_target_pairs={{0,1},{1,0},{2,3},{3,2},{4,5},{5,4},{6,7},{7,6},{8,9},{9,8},{10,11... | collective-permute-start | bytes 1572872 | tf_op jit(solution)/shard_map/ppermute | solution.py:28
  48.1 0.7 copy-start
  50.0 1.4 copy-start.4
  50.1 0.7 copy-start.6
  84.8 29.0 %all-to-all-start.2 = ((f32[16,24,256]{2,1,0:T(8,128)}), f32[16,24,256]{2,1,0:T(8,128)S(1)}, u32[]{:S(2)}, u32[]{:S(2)}) async-start(f32[16,24,256]{2,1,0:T(8,128)} %bitcast.12), calls=%async_computation.2 | async-start | bytes 786432 | tf_op jit(solution)/shard_map/all_to_all | solution.py:144
  113.9 11.7 %all-to-all-start = ((f32[16,16,256]{2,1,0:T(8,128)}), f32[16,16,256]{2,1,0:T(8,128)S(1)}, u32[]{:S(2)}, u32[]{:S(2)}) async-start(f32[16,16,256]{2,1,0:T(8,128)} %bitcast.5), calls=%async_computation | async-start | bytes 524288 | tf_op jit(solution)/shard_map/all_to_all | solution.py:135
  126.3 12.8 %all-to-all-start.3 = ((f32[16,24,256]{2,1,0:T(8,128)}), f32[16,24,256]{2,1,0:T(8,128)S(1)}, u32[]{:S(2)}, u32[]{:S(2)}) async-start(f32[16,24,256]{2,1,0:T(8,128)} %broadcast_in_dim.136), calls=%async_computation.3 | async-start | bytes 786432 | tf_op jit(solution)/shard_map/all_to_all | solution.py:24
  139.9 11.7 %all-to-all-start.1 = ((f32[16,16,256]{2,1,0:T(8,128)}), f32[16,16,256]{2,1,0:T(8,128)S(1)}, u32[]{:S(2)}, u32[]{:S(2)}) async-start(f32[16,16,256]{2,1,0:T(8,128)} %broadcast_in_dim.135), calls=%async_computation.1 | async-start | bytes 524288 | tf_op jit(solution)/shard_map/all_to_all | solution.py:24
  151.8 23.1 %copy-start.2 = (f32[256,256]{0,1:T(8,128)}, f32[256,256]{0,1:T(8,128)S(1)}, u32[]{:S(2)}) copy-start(f32[256,256]{0,1:T(8,128)S(1)} %fusion.25) | copy-start | bytes 786436
  175.3 0.9 slice-start

commit v2 on v0

v2 whole, which is shorter than its diff:
```python
import jax
import jax.numpy as jnp
from jax import lax
from jax.experimental import pallas as pl
from jax.experimental.pallas import tpu as pltpu
from jax.sharding import Mesh
from jax.sharding import PartitionSpec as P

SLOTS = 24
GROUP = 8
PANEL = 128
ROW = ("z", "xh")
HIGHEST = lax.Precision.HIGHEST
F32 = jnp.float32
BF16 = jnp.bfloat16
LIMIT = pltpu.CompilerParams(vmem_limit_bytes=48 * 1024 * 1024)


def iota(shape, dim):
    return lax.broadcasted_iota(jnp.int32, shape, dim)


def contract(a, b, dim_a, dim_b, precision=None):
    return lax.dot_general(
        a, b, (((dim_a,), (dim_b,)), ((), ())), precision=precision, preferred_element_type=F32
    )


def from_everyone(x, axis):
    copies = jnp.broadcast_to(x, (lax.axis_size(axis), *x.shape))
    return lax.all_to_all(copies, axis, split_axis=0, concat_axis=0, tiled=True)


def swapped(x):
    return lax.ppermute(x, "xh", [(0, 1), (1, 0)])


def places(panel_row, rows_dev, holders):
    win = panel_row.shape[1]
    owner = jnp.zeros_like(panel_row)
    for holder in range(1, holders):
        owner = owner + (panel_row >= holder * rows_dev).astype(jnp.int32)
    across = jnp.broadcast_to(owner, (win, win))
    earlier, later = iota((win, win), 0), iota((win, win), 1)
    down = jnp.sum(jnp.where(earlier == later, across, 0), axis=1, keepdims=True)
    same = (across == down) & (earlier < later)
    rank = jnp.sum(same.astype(jnp.int32), axis=0, keepdims=True)
    return owner, rank


def pick_kernel(holders, turn_ref, panel_ref, border_ref, picked_ref, put_ref, rounds_ref):
    rows_dev = border_ref.shape[1]
    z_count = put_ref.shape[0] // SLOTS
    xh = lax.axis_index("xh")
    me = lax.axis_index("z") * 2 + xh
    panel_row = panel_ref[...]
    owner, rank = places(panel_row, rows_dev, holders)
    rounds_ref[0] = jnp.max(rank) + 1
    win = panel_row.shape[1]
    place = rank - turn_ref[0] * SLOTS
    slot = iota((SLOTS, win), 0)
    in_slot = place == slot
    mine = in_slot & (owner == me)
    local = panel_row - me * rows_dev
    source = jnp.sum(jnp.where(mine, local + 1, 0), axis=1, keepdims=True) - 1
    pick = (source == iota((SLOTS, rows_dev), 1)).astype(F32).astype(BF16)
    picked_ref[...] = contract(pick, border_ref[...], 1, 1).astype(BF16)
    put = [
        jnp.where(in_slot & (owner == 2 * holder + xh), 1.0, 0.0) for holder in range(z_count)
    ]
    put_ref[...] = jnp.concatenate(put, axis=0).astype(BF16)


def gather_round(turn, panel_row, border):
    rows_inv, rows_dev = border.shape
    win = panel_row.shape[1]
    z_count = lax.axis_size("z")
    vmem = pl.BlockSpec(memory_space=pltpu.VMEM)
    smem = pl.BlockSpec(memory_space=pltpu.SMEM)
    picked, put, most = pl.pallas_call(
        lambda *refs: pick_kernel(2 * z_count, *refs),
        out_shape=(
            jax.ShapeDtypeStruct((SLOTS, rows_inv), BF16),
            jax.ShapeDtypeStruct((z_count * SLOTS, win), BF16),
            jax.ShapeDtypeStruct((1,), jnp.int32),
        ),
        in_specs=[smem, vmem, vmem],
        out_specs=(vmem, vmem, smem),
        compiler_params=LIMIT,
    )(turn, panel_row, border)
    everyone = lax.all_gather(picked, "z", axis=0, tiled=True)
    return contract(everyone, put, 0, 0).astype(BF16), most[0]


def solve_kernel(own_ref, other_ref, half_ref, panel_ref, barrier_ref, first_ref, out_ref):
    rows_inv = own_ref.shape[0]
    rows_dev, win = first_ref.shape
    xh = lax.axis_index("xh")
    me = lax.axis_index("z") * 2 + xh
    share = win // lax.axis_size("scen")
    half = half_ref[...]
    own = contract(own_ref[...], half, 1, 0)
    other = contract(other_ref[...], half, 1, 0)
    low = jnp.where(xh == 0, own, other)
    high = jnp.where(xh == 0, other, own)
    place = lax.axis_index("scen") * share + iota((share, win), 0)
    on_diagonal = place == iota((share, win), 1)
    local = jnp.sum(jnp.where(on_diagonal, panel_ref[...], 0), axis=1, keepdims=True) - me * rows_dev
    hit = local == iota((share, rows_dev), 1)
    pick = hit.astype(F32)
    base = contract(pick, first_ref[...], 1, 0, HIGHEST)
    term = jnp.sum(jnp.where(hit, barrier_ref[...], 0.0), axis=1, keepdims=True)
    base = base + jnp.where(on_diagonal, term, 0.0)
    first = base.astype(BF16).astype(F32)
    second = (base - first).astype(BF16).astype(F32)
    third = base - first - second
    out_ref[...] = jnp.concatenate([low, high, first, second, third], axis=0).astype(BF16)


def term_kernel(
    own_ref, other_ref, border_ref, gathered_ref, prob_ref, slot_ref, out_ref, base_ref
):
    z_count, lines, win = gathered_ref.shape
    rows_inv = border_ref.shape[0]
    rows_dev = border_ref.shape[1]
    scen_count, per_scen, _ = out_ref.shape
    share = win // scen_count
    step = rows_inv // z_count
    solved = gathered_ref[:, :step, :].reshape(rows_inv, win)
    match = iota(prob_ref.shape, 1) == slot_ref[...]
    weight = jnp.sum(jnp.where(match, prob_ref[...], 0.0), axis=1, keepdims=True)
    columns = own_ref[...] + other_ref[...]
    block = contract(columns, solved, 0, 0) * weight
    out_ref[:, :share, :] = block.reshape(scen_count, share, win)
    term = contract(border_ref[...], solved, 0, 0) * weight
    out_ref[:, share:, :] = term.reshape(scen_count, per_scen - share, win)
    parts = jnp.sum(gathered_ref[:, step:, :].astype(F32), axis=0)
    base_ref[...] = parts[:share] + parts[share : 2 * share] + parts[2 * share :]


def inverse_factor(symmetric):
    size = symmetric.shape[0]
    count = size // GROUP
    work = [symmetric[GROUP * i : GROUP * (i + 1), :] for i in range(count)]
    lane, sub = iota((GROUP, size), 1), iota((GROUP, size), 0)
    result = []
    for group in range(count):
        low = group * GROUP
        block = work[group]
        inside = (lane >= low) & (lane < low + GROUP)
        lower = [[None] * GROUP for _ in range(GROUP)]
        scale = [None] * GROUP
        entry = [
            [jnp.broadcast_to(block[i : i + 1, low + j : low + j + 1], block.shape) for j in range(i + 1)]
            for i in range(GROUP)
        ]
        for j in range(GROUP):
            pivot = entry[j][j]
            for t in range(j):
                pivot = pivot - lower[j][t] * lower[j][t]
            scale[j] = lax.rsqrt(pivot)
            for i in range(j + 1, GROUP):
                value = entry[i][j]
                for t in range(j):
                    value = value - lower[i][t] * lower[j][t]
                lower[i][j] = value * scale[j]
        forward = []
        for i in range(GROUP):
            row = jnp.broadcast_to(block[i : i + 1, :], block.shape)
            row = jnp.where(inside, jnp.where(lane == low + i, 1.0, 0.0), row)
            for j in range(i):
                row = row - lower[i][j] * forward[j]
            forward.append(row * scale[i])
        done = forward[0]
        for i in range(1, GROUP):
            done = jnp.where(sub == i, forward[i], done)
        result.append(jnp.where(lane <= sub + low, done, 0.0))
        if group + 1 == count:
            break
        back = [None] * GROUP
        for i in reversed(range(GROUP)):
            row = forward[i]
            for j in range(i + 1, GROUP):
                row = row - lower[j][i] * back[j]
            back[i] = row * scale[i]
        for later in range(group + 1, count):
            old = work[later]
            new = jnp.where(inside, 0.0, old)
            for j in range(GROUP):
                new = new - old[:, low + j : low + j + 1] * back[j]
            work[later] = new
    return jnp.concatenate(result, axis=0)


def factor_kernel(gathered_ref, base_ref, out_ref):
    scen_count, per_scen, win = gathered_ref.shape
    share = win // scen_count
    diag = gathered_ref[:, :share, :].reshape(win, win)
    rows = gathered_ref[:, share:, :].reshape(base_ref.shape) + base_ref[...]

    def symmetric(i, j):
        one = diag[i : i + PANEL, j : j + PANEL]
        other = diag[j : j + PANEL, i : i + PANEL]
        return 0.5 * (one + other.T)

    first = inverse_factor(symmetric(0, 0))
    across = contract(symmetric(PANEL, 0), first, 1, 1, HIGHEST)
    second = inverse_factor(symmetric(PANEL, PANEL) - contract(across, across, 1, 1, HIGHEST))
    left = contract(rows[:, :PANEL], first, 1, 1, HIGHEST)
    right = rows[:, PANEL:] - contract(left, across, 1, 1, HIGHEST)
    out_ref[:, :PANEL] = left
    out_ref[:, PANEL:] = contract(right, second, 1, 1, HIGHEST)


def per_device(borders, kkt_inverse, first_section, barrier, panel_vars, probability, assignment):
    border, inverse_rows = borders[0], kkt_inverse[0]
    rows_inv, rows_dev = border.shape
    win = first_section.shape[1]
    scen_count = lax.axis_size("scen")
    me_row = lax.axis_index("z") * 2 + lax.axis_index("xh")
    panel_row = panel_vars[None, :]

    other_rows = swapped(inverse_rows)
    half, most = gather_round(jnp.zeros((1,), jnp.int32), panel_row, border)
    _, half = lax.while_loop(
        lambda state: state[0] * SLOTS < most,
        lambda state: (
            state[0] + 1,
            state[1] + gather_round(state[0][None], panel_row, border)[0],
        ),
        (jnp.int32(1), half),
    )
    other_half = swapped(half)

    share = win // scen_count
    own_lines = 2 * inverse_rows.shape[0]
    message = pl.pallas_call(
        solve_kernel,
        out_shape=jax.ShapeDtypeStruct((own_lines + 3 * share, win), BF16),
        compiler_params=LIMIT,
    )(inverse_rows, other_rows, half, panel_row, barrier[None, :], first_section)
    both = lax.all_gather(message, "xh", axis=0)
    gathered = lax.all_gather(both[0] + both[1], "z", axis=0)

    per_scen = share + rows_dev // scen_count
    terms, base = pl.pallas_call(
        term_kernel,
        out_shape=(
            jax.ShapeDtypeStruct((scen_count, per_scen, win), F32),
            jax.ShapeDtypeStruct((share, win), F32),
        ),
        compiler_params=LIMIT,
    )(half, other_half, border, gathered, probability[None, :], assignment[None, :])
    shares = lax.all_to_all(terms, "scen", 0, 0, tiled=True)
    summed = jnp.sum(shares, axis=0) + jnp.pad(base, ((0, per_scen - share), (0, 0)))
    everyone = from_everyone(summed, "scen")

    hits = (
        jnp.arange(rows_dev, dtype=jnp.int32)[:, None] + me_row * rows_dev == panel_vars[None, :]
    )
    rows_base = first_section + jnp.where(hits, barrier[:, None], 0.0)
    return pl.pallas_call(
        factor_kernel,
        out_shape=jax.ShapeDtypeStruct((rows_dev, win), F32),
        compiler_params=LIMIT,
    )(everyone, rows_base)


def solution(mesh):
    torus = Mesh(mesh.devices.reshape(mesh.shape["scen"], 16, 2), ("scen", "z", "xh"))
    return jax.shard_map(
        per_device,
        mesh=torus,
        in_specs=(
            P("scen", None, ROW),
            P("scen", ROW, None),
            P(ROW, None),
            P(ROW),
            P(),
            P(),
            P("scen"),
        ),
        out_specs=P(ROW, None),
        check_vma=False,
    )
```

time: 707 us -> 143 us (0.20)
  waiting for transfers between devices: 559 us -> 11.2 us
  blocking collectives: 47 us -> 98.9 us
  other arithmetic: 48.4 us -> 0.23 us
  Pallas kernels: 0 us -> 15.9 us
  between operations: 14.1 us -> 0.78 us
  starting transfers between devices: 24.6 us -> 11.6 us
  local copies, waits for them, and re-layouts: 10.8 us -> 2.89 us
    psum x1 -> x0, waiting for transfers between devices: 441 us -> none  [per_device(): diag_block = lax.psum(own_block, SCEN_ROW)]
    reduce_scatter x2 -> x0, waiting for transfers between devices: 96.3 us -> none  [own_block_2(): blocks = lax.psum_scatter(blocks, axes[k], scatter_dimension=0, tiled=True)]
    another operation x10 -> x0, other arithmetic: 45.9 us -> none  [the longest x6 24.9 us: factorize(): panel_chol = jnp.linalg.cholesky(block_cols[low_col:high_col, :])]
    all_gather x2 -> x3, blocking collectives: 31.8 us -> 67 us  [the longest x1 33.2 us: gather_round(): everyone = lax.all_gather(picked, 'z', axis=0, tiled=True)]
    all_to_all x1, blocking collectives: 15.3 us -> 31.9 us  [per_device(): shares = lax.all_to_all(terms, 'scen', 0, 0, tiled=True)]
    pallas_call x0 -> x4, Pallas kernels: none -> 15.9 us  [the longest x1 12.8 us: per_device(): pl.pallas_call(factor_kernel, out_shape=jax.ShapeDtypeStruct((rows_dev, w...]
    all_to_all x1 -> x0, starting transfers between devices: 15.9 us -> none  [summed_on_arrival(): blocks = lax.all_to_all(split_up(x, dim, length), axis, 0, 0, tiled=True)]
    all_to_all x1, waiting for transfers between devices: 21 us -> 11.1 us  [from_everyone(): return lax.all_to_all(copies, axis, split_axis=0, concat_axis=0, tiled=True)]
  transfers between devices with their start and end apart: 5 -> 3, of which waited for: 4 -> 1; matrix products, arithmetic and copies ran while one was open for 7% -> 0% of each run, Pallas kernels for 0% -> 2%
where the time goes in v2:
time: 143 us
  blocking collectives  98.9 us (69%)
  Pallas kernels  15.9 us (11%)
  starting transfers between devices  11.6 us (8%)
  waiting for transfers between devices  11.2 us (8%)
  local copies, waits for them, and re-layouts  2.89 us (2%)
    all_gather x1, blocking collectives, gather_round(): everyone = lax.all_gather(picked, 'z', axis=0, tiled=True)  33.2 us
    all_to_all x1, blocking collectives, per_device(): shares = lax.all_to_all(terms, 'scen', 0, 0, tiled=True)  31.9 us
    all_gather x1, blocking collectives, per_device(): gathered = lax.all_gather(both[0] + both[1], 'z', axis=0)  25.1 us
    pallas_call x1, Pallas kernels, per_device(): pl.pallas_call(factor_kernel, out_shape=jax.ShapeDtypeStruct((rows_dev, w...  12.8 us
    all_to_all x1, waiting for transfers between devices, from_everyone(): return lax.all_to_all(copies, axis, split_axis=0, concat_axis=0, tiled=True)  11.1 us
    all_gather x1, blocking collectives, per_device(): both = lax.all_gather(message, 'xh', axis=0)  8.72 us
    ppermute x2, starting transfers between devices, swapped(): return lax.ppermute(x, 'xh', [(0, 1), (1, 0)])  7.6 us
    all_to_all x1, starting transfers between devices, from_everyone(): return lax.all_to_all(copies, axis, split_axis=0, concat_axis=0, tiled=True)  4.04 us
  transfers between devices with their start and end apart: 3, of which 1 were waited for; matrix products, arithmetic and copies ran while one was open for 0% of the time, Pallas kernels for 2%

profile of v2, /device:TPU:1, one launch (start us, length us, event | category | flops | bytes accessed | tf_op | source)
XLA Modules:
  0.0 142.7 jit_solution(365163144272973061)
XLA Ops:
  0.0 5.5 %collective-permute-start.1 = (bf16[32,1024]{1,0:T(8,128)(2,1)}, bf16[32,1024]{1,0:T(8,128)(2,1)S(1)}, u32[]{:S(2)}, u32[]{:S(2)}) collective-permute-start(bf16[32,1024]{1,0:T(8,128)(2,1)} %bitcast.20), channel_id=1, source_target_pairs={{0,1},{1,0},{2,3},{3,2},{4,5},{5,4},{6,7},{7,6},{8,9},{9,8},{10,11... | collective-permute-start | bytes 196616 | tf_op jit(solution)/shard_map/ppermute | solution.py:35
  5.5 0.0 copy-start.4
  5.5 0.7 copy-done.4
  6.2 2.1 %shard_map.73 = (bf16[24,1024]{1,0:T(8,128)(2,1)S(1)}, bf16[384,256]{1,0:T(8,128)(2,1)S(1)}, s32[1]{0:T(128)}) custom-call(s32[1]{0:T(128)} %constant.6.clone.1.refs_0_, s32[1,256]{1,0:T(1,128)S(1)} %bitcast.25, bf16[1024,384]{1,0:T(8,128)(2,1)} %bitcast.23), custom_call_target="tpu_custom_call" | custom-call | tf_op jit(solution)/shard_map/pallas_call | solution.py:80
  8.2 33.2 %all_gather.16 = bf16[384,1024]{1,0:T(8,128)(2,1)S(1)} all-gather(bf16[24,1024]{1,0:T(8,128)(2,1)S(1)} %get-tuple-element.40), channel_id=1, replica_groups=mesh['scen'=16,'z'=16,'xh'=2] {'z'}, dimensions={0}, use_global_device_ids=true | all-gather | bytes 835584 | tf_op jit(solution)/shard_map/all_gather | solution.py:91
  41.4 0.5 convolution_convert_fusion.1
  41.9 0.7 copy-done.3
  42.5 0.7 while.10
  43.2 2.1 %collective-permute-start = (bf16[1024,256]{1,0:T(8,128)(2,1)S(1)}, bf16[1024,256]{1,0:T(8,128)(2,1)S(1)}, u32[]{:S(2)}, u32[]{:S(2)}) collective-permute-start(bf16[1024,256]{1,0:T(8,128)(2,1)S(1)} %get-tuple-element.43.half_ref.own_ref), channel_id=1, source_target_pairs={{0,1},{1,0},{2,3},{3,2},{4,5},{5,4},{6,7},{7,6},{8,9},{9,8},{10,11... | collective-permute-start | bytes 1572872 | tf_op jit(solution)/shard_map/ppermute | solution.py:35
  45.4 0.0 copy-done.5
  46.0 0.0 collective-permute-done.1.other_ref
  46.1 0.0 copy-done
  46.1 0.5 shard_map.74
  46.6 8.7 %all-gather = bf16[224,256]{1,0:T(8,128)(2,1)S(1)} all-gather(bf16[112,256]{1,0:T(8,128)(2,1)S(1)} %shard_map.74), channel_id=2, replica_groups=mesh['scen'=16,'z'=16,'xh'=2] {'xh'}, dimensions={0}, use_global_device_ids=true | all-gather | bytes 172032 | tf_op jit(solution)/shard_map/all_gather | solution.py:242
  55.3 25.1 %all-gather.1 = bf16[1792,256]{1,0:T(8,128)(2,1)S(1)} all-gather(bf16[112,256]{1,0:T(8,128)(2,1)S(1)} %slice_add_fusion), channel_id=3, replica_groups=mesh['scen'=16,'z'=16,'xh'=2] {'z'}, dimensions={0}, use_global_device_ids=true | all-gather | bytes 974848 | tf_op jit(solution)/shard_map/all_gather | solution.py:243
  80.4 0.0 collective-permute-done.other_ref
  80.4 0.7 copy-done.2
  81.1 0.6 shard_map.75
  81.7 31.9 %all_to_all.10 = f32[16,40,256]{2,1,0:T(8,128)S(1)} all-to-all(f32[16,40,256]{2,1,0:T(8,128)S(1)} %get-tuple-element.44), channel_id=1, replica_groups=mesh['scen'=16,'z'=16,'xh'=2] {'scen'}, dimensions={0} | all-to-all | bytes 1310720 | tf_op jit(solution)/shard_map/all_to_all | solution.py:254
  113.7 0.9 broadcast_in_dim.37
  114.6 4.0 %all-to-all-start.1 = ((f32[16,40,256]{2,1,0:T(8,128)}), f32[16,40,256]{2,1,0:T(8,128)S(1)}, u32[]{:S(2)}, u32[]{:S(2)}) async-start(f32[16,40,256]{2,1,0:T(8,128)} %broadcast_in_dim.37), calls=%async_computation.1 | async-start | bytes 1310720 | tf_op jit(solution)/shard_map/all_to_all | solution.py:31
  118.6 0.2 select_add_fusion.base_ref
  118.8 11.1 %all-to-all-done.1.gathered_ref = f32[16,40,256]{2,1,0:T(8,128)S(1)} async-done(((f32[16,40,256]{2,1,0:T(8,128)}), f32[16,40,256]{2,1,0:T(8,128)S(1)}, u32[]{:S(2)}, u32[]{:S(2)}) %all-to-all-start.1) | async-done | bytes 655392 | tf_op jit(solution)/shard_map/all_to_all | solution.py:31
  129.9 12.8 %shard_map.76 = f32[384,256]{1,0:T(8,128)} custom-call(f32[16,40,256]{2,1,0:T(8,128)S(1)} %all-to-all-done.1.gathered_ref, f32[384,256]{1,0:T(8,128)S(1)} %select_add_fusion.base_ref), custom_call_target="tpu_custom_call" | custom-call | tf_op jit(solution)/shard_map/pallas_call | solution.py:262
  (11 shorter events, 0.1 us)
Async XLA Ops:
  0.0 46.0 %collective-permute-start.1 = (bf16[32,1024]{1,0:T(8,128)(2,1)}, bf16[32,1024]{1,0:T(8,128)(2,1)S(1)}, u32[]{:S(2)}, u32[]{:S(2)}) collective-permute-start(bf16[32,1024]{1,0:T(8,128)(2,1)} %bitcast.20), channel_id=1, source_target_pairs={{0,1},{1,0},{2,3},{3,2},{4,5},{5,4},{6,7},{7,6},{8,9},{9,8},{10,11... | collective-permute-start | bytes 196616 | tf_op jit(solution)/shard_map/ppermute | solution.py:35
  5.5 0.7 copy-start.4
  41.4 1.1 copy-start.3
  42.5 2.8 %copy-start.5 = (f32[384]{0:T(512)S(1)}, f32[384]{0:T(512)}, u32[]{:S(2)}) copy-start(f32[384]{0:T(512)} %param.12) | copy-start | bytes 4612
  42.5 3.5 %copy-start = (f32[384,256]{1,0:T(8,128)S(1)}, f32[384,256]{1,0:T(8,128)}, u32[]{:S(2)}) copy-start(f32[384,256]{1,0:T(8,128)} %first_ref.1) | copy-start | bytes 1179652
  42.5 3.5 %copy-start.1 = (bf16[1,32,1024]{2,1,0:T(8,128)(2,1)S(1)}, bf16[1,32,1024]{2,1,0:T(8,128)(2,1)}, u32[]{:S(2)}) copy-start(bf16[1,32,1024]{2,1,0:T(8,128)(2,1)} %param.10) | copy-start | bytes 196612
  43.2 37.2 %collective-permute-start = (bf16[1024,256]{1,0:T(8,128)(2,1)S(1)}, bf16[1024,256]{1,0:T(8,128)(2,1)S(1)}, u32[]{:S(2)}, u32[]{:S(2)}) collective-permute-start(bf16[1024,256]{1,0:T(8,128)(2,1)S(1)} %get-tuple-element.43.half_ref.own_ref), channel_id=1, source_target_pairs={{0,1},{1,0},{2,3},{3,2},{4,5},{5,4},{6,7},{7,6},{8,9},{9,8},{10,11... | collective-permute-start | bytes 1572872 | tf_op jit(solution)/shard_map/ppermute | solution.py:35
  80.4 0.7 copy-start.2
  114.6 15.4 %all-to-all-start.1 = ((f32[16,40,256]{2,1,0:T(8,128)}), f32[16,40,256]{2,1,0:T(8,128)S(1)}, u32[]{:S(2)}, u32[]{:S(2)}) async-start(f32[16,40,256]{2,1,0:T(8,128)} %broadcast_in_dim.37), calls=%async_computation.1 | async-start | bytes 1310720 | tf_op jit(solution)/shard_map/all_to_all | solution.py:31

commit v3 on v2

--- a/solution.py
+++ b/solution.py
@@ -9,7 +9,9 @@
 SLOTS = 24
 GROUP = 8
 PANEL = 128
-ROW = ("z", "xh")
+Z = ("zh", "zl")
+ROW = ("zh", "zl", "xh")
+FAR = ("zh", "xh")
 HIGHEST = lax.Precision.HIGHEST
 F32 = jnp.float32
 BF16 = jnp.bfloat16
@@ -48,11 +50,15 @@
     return owner, rank
 
 
+def my_row():
+    return (lax.axis_index("zh") * lax.axis_size("zl") + lax.axis_index("zl")) * 2 + lax.axis_index("xh")
+
+
 def pick_kernel(holders, turn_ref, panel_ref, border_ref, picked_ref, put_ref, rounds_ref):
     rows_dev = border_ref.shape[1]
     z_count = put_ref.shape[0] // SLOTS
     xh = lax.axis_index("xh")
-    me = lax.axis_index("z") * 2 + xh
+    me = my_row()
     panel_row = panel_ref[...]
     owner, rank = places(panel_row, rows_dev, holders)
     rounds_ref[0] = jnp.max(rank) + 1
@@ -74,7 +80,7 @@
 def gather_round(turn, panel_row, border):
     rows_inv, rows_dev = border.shape
     win = panel_row.shape[1]
-    z_count = lax.axis_size("z")
+    z_count = lax.axis_size(Z)
     vmem = pl.BlockSpec(memory_space=pltpu.VMEM)
     smem = pl.BlockSpec(memory_space=pltpu.SMEM)
     picked, put, most = pl.pallas_call(
@@ -88,45 +94,65 @@
         out_specs=(vmem, vmem, smem),
         compiler_params=LIMIT,
     )(turn, panel_row, border)
-    everyone = lax.all_gather(picked, "z", axis=0, tiled=True)
+    everyone = lax.all_gather(picked, Z, axis=0, tiled=True)
     return contract(everyone, put, 0, 0).astype(BF16), most[0]
 
 
-def solve_kernel(own_ref, other_ref, half_ref, panel_ref, barrier_ref, first_ref, out_ref):
-    rows_inv = own_ref.shape[0]
+def base_kernel(panel_ref, barrier_ref, first_ref, inverse_ref, out_ref):
+    copies, lines, rows_inv = out_ref.shape
+    own = inverse_ref.shape[0]
     rows_dev, win = first_ref.shape
-    xh = lax.axis_index("xh")
-    me = lax.axis_index("z") * 2 + xh
     share = win // lax.axis_size("scen")
-    half = half_ref[...]
-    own = contract(own_ref[...], half, 1, 0)
-    other = contract(other_ref[...], half, 1, 0)
-    low = jnp.where(xh == 0, own, other)
-    high = jnp.where(xh == 0, other, own)
     place = lax.axis_index("scen") * share + iota((share, win), 0)
     on_diagonal = place == iota((share, win), 1)
-    local = jnp.sum(jnp.where(on_diagonal, panel_ref[...], 0), axis=1, keepdims=True) - me * rows_dev
-    hit = local == iota((share, rows_dev), 1)
-    pick = hit.astype(F32)
-    base = contract(pick, first_ref[...], 1, 0, HIGHEST)
+    local = jnp.sum(jnp.where(on_diagonal, panel_ref[...], 0), axis=1, keepdims=True)
+    hit = local - my_row() * rows_dev == iota((share, rows_dev), 1)
+    base = contract(hit.astype(F32), first_ref[...], 1, 0, HIGHEST)
     term = jnp.sum(jnp.where(hit, barrier_ref[...], 0.0), axis=1, keepdims=True)
     base = base + jnp.where(on_diagonal, term, 0.0)
-    first = base.astype(BF16).astype(F32)
-    second = (base - first).astype(BF16).astype(F32)
-    third = base - first - second
-    out_ref[...] = jnp.concatenate([low, high, first, second, third], axis=0).astype(BF16)
+    rounded = base.astype(BF16).astype(F32)
+    rest = base - rounded
+    fold = rows_inv // win
+    step = share // fold
+    lanes = [
+        jnp.concatenate([part[step * i : step * (i + 1)] for i in range(fold)], axis=1)
+        for part in (rounded, rest)
+    ]
+    message = jnp.concatenate([inverse_ref[...].astype(F32), *lanes], axis=0).astype(BF16)
+    out_ref[...] = jnp.broadcast_to(message[None], out_ref.shape)
+
+
+def solve_kernel(far_ref, half_ref, out_ref, base_ref):
+    copies, lines, rows_inv = far_ref.shape
+    win = half_ref.shape[1]
+    extra = base_ref.shape[0] * win // rows_inv
+    own = lines - extra
+    far = far_ref[...].astype(F32)
+    rows = far[:, :own, :].reshape(copies * own, rows_inv).astype(BF16)
+    out_ref[...] = contract(rows, half_ref[...], 1, 0).astype(BF16)
+    parts = jnp.sum(far[:, own:, :], axis=0)
+    fold = rows_inv // win
+    step = extra // 2
+    lanes = [
+        parts[step * p : step * (p + 1), win * i : win * (i + 1)] for p in range(2) for i in range(fold)
+    ]
+    base_ref[...] = jnp.concatenate(lanes, axis=0).astype(BF16)
 
 
 def term_kernel(
-    own_ref, other_ref, border_ref, gathered_ref, prob_ref, slot_ref, out_ref, base_ref
+    own_ref, other_ref, border_ref, gathered_ref, prob_ref, slot_ref, out_ref, base_ref, solved_ref
 ):
-    z_count, lines, win = gathered_ref.shape
+    near, lines, win = gathered_ref.shape
     rows_inv = border_ref.shape[0]
-    rows_dev = border_ref.shape[1]
     scen_count, per_scen, _ = out_ref.shape
     share = win // scen_count
-    step = rows_inv // z_count
-    solved = gathered_ref[:, :step, :].reshape(rows_inv, win)
+    held = rows_inv // near
+    step = held // lax.axis_size("zh")
+    for low in range(near):
+        for high in range(held // step):
+            at = (high * near + low) * step
+            solved_ref[at : at + step, :] = gathered_ref[low, high * step : (high + 1) * step, :]
+    solved = solved_ref[...]
     match = iota(prob_ref.shape, 1) == slot_ref[...]
     weight = jnp.sum(jnp.where(match, prob_ref[...], 0.0), axis=1, keepdims=True)
     columns = own_ref[...] + other_ref[...]
@@ -134,8 +160,8 @@
     out_ref[:, :share, :] = block.reshape(scen_count, share, win)
     term = contract(border_ref[...], solved, 0, 0) * weight
     out_ref[:, share:, :] = term.reshape(scen_count, per_scen - share, win)
-    parts = jnp.sum(gathered_ref[:, step:, :].astype(F32), axis=0)
-    base_ref[...] = parts[:share] + parts[share : 2 * share] + parts[2 * share :]
+    parts = jnp.sum(gathered_ref[:, held:, :].astype(F32), axis=0)
+    base_ref[...] = parts[:share] + parts[share:]
 
 
 def inverse_factor(symmetric):
@@ -217,10 +243,18 @@
     rows_inv, rows_dev = border.shape
     win = first_section.shape[1]
     scen_count = lax.axis_size("scen")
-    me_row = lax.axis_index("z") * 2 + lax.axis_index("xh")
+    share = win // scen_count
+    own_rows = inverse_rows.shape[0]
     panel_row = panel_vars[None, :]
 
-    other_rows = swapped(inverse_rows)
+    far_count = lax.axis_size(FAR)
+    far_lines = own_rows + 2 * share * win // rows_inv
+    far = pl.pallas_call(
+        base_kernel,
+        out_shape=jax.ShapeDtypeStruct((far_count, far_lines, rows_inv), BF16),
+        compiler_params=LIMIT,
+    )(panel_row, barrier[None, :], first_section, inverse_rows)
+    far = lax.all_to_all(far, FAR, 0, 0, tiled=True)
     half, most = gather_round(jnp.zeros((1,), jnp.int32), panel_row, border)
     _, half = lax.while_loop(
         lambda state: state[0] * SLOTS < most,
@@ -230,17 +264,20 @@
         ),
         (jnp.int32(1), half),
     )
+
+    solved, base = pl.pallas_call(
+        solve_kernel,
+        out_shape=(
+            jax.ShapeDtypeStruct((far_count * own_rows, win), BF16),
+            jax.ShapeDtypeStruct((2 * share, win), BF16),
+        ),
+        compiler_params=LIMIT,
+    )(far, half)
+    both = lax.all_gather(solved, "xh", axis=0)
+    both, half = lax.optimization_barrier((both, half))
     other_half = swapped(half)
-
-    share = win // scen_count
-    own_lines = 2 * inverse_rows.shape[0]
-    message = pl.pallas_call(
-        solve_kernel,
-        out_shape=jax.ShapeDtypeStruct((own_lines + 3 * share, win), BF16),
-        compiler_params=LIMIT,
-    )(inverse_rows, other_rows, half, panel_row, barrier[None, :], first_section)
-    both = lax.all_gather(message, "xh", axis=0)
-    gathered = lax.all_gather(both[0] + both[1], "z", axis=0)
+    message = jnp.concatenate([both[0] + both[1], base], axis=0)
+    gathered = lax.all_gather(message, "zl", axis=0)
 
     per_scen = share + rows_dev // scen_count
     terms, base = pl.pallas_call(
@@ -249,6 +286,7 @@
             jax.ShapeDtypeStruct((scen_count, per_scen, win), F32),
             jax.ShapeDtypeStruct((share, win), F32),
         ),
+        scratch_shapes=[pltpu.VMEM((rows_inv, win), BF16)],
         compiler_params=LIMIT,
     )(half, other_half, border, gathered, probability[None, :], assignment[None, :])
     shares = lax.all_to_all(terms, "scen", 0, 0, tiled=True)
@@ -256,7 +294,7 @@
     everyone = from_everyone(summed, "scen")
 
     hits = (
-        jnp.arange(rows_dev, dtype=jnp.int32)[:, None] + me_row * rows_dev == panel_vars[None, :]
+        jnp.arange(rows_dev, dtype=jnp.int32)[:, None] + my_row() * rows_dev == panel_vars[None, :]
     )
     rows_base = first_section + jnp.where(hits, barrier[:, None], 0.0)
     return pl.pallas_call(
@@ -267,7 +305,7 @@
 
 
 def solution(mesh):
-    torus = Mesh(mesh.devices.reshape(mesh.shape["scen"], 16, 2), ("scen", "z", "xh"))
+    torus = Mesh(mesh.devices.reshape(mesh.shape["scen"], 4, 4, 2), ("scen", "zh", "zl", "xh"))
     return jax.shard_map(
         per_device,
         mesh=torus,

time: 143 us -> 162 us (1.13)
  starting transfers between devices: 11.6 us -> 27.3 us
  local copies, waits for them, and re-layouts: 2.89 us -> 5.4 us
    all_to_all x0 -> x1, starting transfers between devices: none -> 18.2 us  [per_device(): far = lax.all_to_all(far, FAR, 0, 0, tiled=True)]
    all_gather x3, blocking collectives: 67 us -> 71.1 us  [the longest x1 52 us: gather_round(): everyone = lax.all_gather(picked, Z, axis=0, tiled=True)]
    all_to_all x1, blocking collectives: 31.9 us -> 28.9 us  [per_device(): shares = lax.all_to_all(terms, 'scen', 0, 0, tiled=True)]
    ppermute x2 -> x1, starting transfers between devices: 7.6 us -> 4.88 us  [swapped(): return lax.ppermute(x, 'xh', [(0, 1), (1, 0)])]
    unnamed x12 -> x14, local copies, waits for them, and re-layouts: 2 us -> 3.83 us
  transfers between devices with their start and end apart: 3 -> 3, of which waited for: 1 -> 1; matrix products, arithmetic and copies ran while one was open for 0% -> 0% of each run, Pallas kernels for 2% -> 1%
where the time goes in v3:
time: 162 us; the launch traced here: 161 us
  blocking collectives  100 us (62%)
  starting transfers between devices  27.3 us (17%)
  Pallas kernels  15.8 us (10%)
  waiting for transfers between devices  10.5 us (6%)
  local copies, waits for them, and re-layouts  5.4 us (3%)
    all_gather x1, blocking collectives, gather_round(): everyone = lax.all_gather(picked, Z, axis=0, tiled=True)  52 us
    all_to_all x1, blocking collectives, per_device(): shares = lax.all_to_all(terms, 'scen', 0, 0, tiled=True)  28.9 us
    all_to_all x1, starting transfers between devices, per_device(): far = lax.all_to_all(far, FAR, 0, 0, tiled=True)  18.2 us
    pallas_call x1, Pallas kernels, per_device(): pl.pallas_call(factor_kernel, out_shape=jax.ShapeDtypeStruct((rows_dev, w...  12.8 us
    all_gather x1, blocking collectives, per_device(): gathered = lax.all_gather(message, 'zl', axis=0)  12.6 us
    all_to_all x1, waiting for transfers between devices, from_everyone(): return lax.all_to_all(copies, axis, split_axis=0, concat_axis=0, tiled=True)  10.5 us
    all_gather x1, blocking collectives, per_device(): both = lax.all_gather(solved, 'xh', axis=0)  6.47 us
    ppermute x1, starting transfers between devices, swapped(): return lax.ppermute(x, 'xh', [(0, 1), (1, 0)])  4.88 us
  transfers between devices with their start and end apart: 3, of which 1 were waited for; matrix products, arithmetic and copies ran while one was open for 0% of the time, Pallas kernels for 1%

profile of v3, /device:TPU:1, one launch (start us, length us, event | category | flops | bytes accessed | tf_op | source)
XLA Modules:
  0.0 161.1 jit_solution(14498667448473426630)
XLA Ops:
  0.0 0.7 broadcast_in_dim.34.barrier_ref
  0.7 0.7 copy-done.5
  1.4 1.0 copy-done
  2.4 0.8 copy-done.2
  3.2 1.2 shard_map.73
  4.4 18.2 %all-to-all-start = ((bf16[8,40,1024]{2,1,0:T(8,128)(2,1)}), bf16[8,40,1024]{2,1,0:T(8,128)(2,1)S(1)}, u32[]{:S(2)}, u32[]{:S(2)}) async-start(bf16[8,40,1024]{2,1,0:T(8,128)(2,1)} %shard_map.73), calls=%async_computation | async-start | bytes 1310720 | tf_op jit(solution)/shard_map/all_to_all | solution.py:257
  22.6 0.9 shard_map.74
  23.6 52.0 %all_gather.18 = bf16[384,1024]{1,0:T(8,128)(2,1)S(1)} all-gather(bf16[24,1024]{1,0:T(8,128)(2,1)S(1)} %get-tuple-element.44), channel_id=1, replica_groups=mesh['scen'=16,'zh'=4,'zl'=4,'xh'=2] {'zh','zl'}, dimensions={0}, use_global_device_ids=true | all-gather | bytes 835584 | tf_op jit(solution)/shard_map/all_gather | solution.py:97
  76.3 0.5 convolution_convert_fusion.1
  76.8 0.6 while.10
  77.4 0.0 all-to-all-done.far_ref
  77.4 0.3 shard_map.75
  77.7 6.5 %all-gather = bf16[512,256]{1,0:T(8,128)(2,1)S(1)} all-gather(bf16[256,256]{1,0:T(8,128)(2,1)S(1)} %get-tuple-element.48), channel_id=2, replica_groups=mesh['scen'=16,'zh'=4,'zl'=4,'xh'=2] {'xh'}, dimensions={0}, use_global_device_ids=true | all-gather | bytes 393216 | tf_op jit(solution)/shard_map/all_gather | solution.py:276
  84.2 4.9 %collective-permute-start = (bf16[1024,256]{1,0:T(8,128)(2,1)S(1)}, bf16[1024,256]{1,0:T(8,128)(2,1)S(1)}, u32[]{:S(2)}, u32[]{:S(2)}) collective-permute-start(bf16[1024,256]{1,0:T(8,128)(2,1)S(1)} %get-tuple-element.49.half_ref.own_ref), channel_id=1, source_target_pairs={{0,1},{1,0},{2,3},{3,2},{4,5},{5,4},{6,7},{7,6},{8,9},{9,8},{10,11... | collective-permute-start | bytes 1572872 | tf_op jit(solution)/shard_map/ppermute | solution.py:37
  89.1 12.6 %all-gather.1 = bf16[1152,256]{1,0:T(8,128)(2,1)S(1)} all-gather(bf16[288,256]{1,0:T(8,128)(2,1)S(1)} %pad_maximum_fusion), channel_id=3, replica_groups=mesh['scen'=16,'zh'=4,'zl'=4,'xh'=2] {'zl'}, dimensions={0}, use_global_device_ids=true | all-gather | bytes 737280 | tf_op jit(solution)/shard_map/all_gather | solution.py:280
  101.7 0.7 copy-done.3
  102.4 0.6 shard_map.76
  102.9 28.9 %all_to_all.15 = f32[16,40,256]{2,1,0:T(8,128)S(1)} all-to-all(f32[16,40,256]{2,1,0:T(8,128)S(1)} %get-tuple-element.52), channel_id=1, replica_groups=mesh['scen'=16,'zh'=4,'zl'=4,'xh'=2] {'scen'}, dimensions={0} | all-to-all | bytes 1310720 | tf_op jit(solution)/shard_map/all_to_all | solution.py:292
  131.9 0.9 broadcast_in_dim.37
  132.8 4.2 %all-to-all-start.2 = ((f32[16,40,256]{2,1,0:T(8,128)}), f32[16,40,256]{2,1,0:T(8,128)S(1)}, u32[]{:S(2)}, u32[]{:S(2)}) async-start(f32[16,40,256]{2,1,0:T(8,128)} %broadcast_in_dim.37), calls=%async_computation.2 | async-start | bytes 1310720 | tf_op jit(solution)/shard_map/all_to_all | solution.py:33
  137.0 0.7 copy-done.6
  137.7 0.2 select_add_fusion.base_ref
  137.8 10.5 %all-to-all-done.2.gathered_ref = f32[16,40,256]{2,1,0:T(8,128)S(1)} async-done(((f32[16,40,256]{2,1,0:T(8,128)}), f32[16,40,256]{2,1,0:T(8,128)S(1)}, u32[]{:S(2)}, u32[]{:S(2)}) %all-to-all-start.2) | async-done | bytes 655392 | tf_op jit(solution)/shard_map/all_to_all | solution.py:33
  148.3 12.8 %shard_map.77 = f32[384,256]{1,0:T(8,128)} custom-call(f32[16,40,256]{2,1,0:T(8,128)S(1)} %all-to-all-done.2.gathered_ref, f32[384,256]{1,0:T(8,128)S(1)} %select_add_fusion.base_ref), custom_call_target="tpu_custom_call" | custom-call | tf_op jit(solution)/shard_map/pallas_call | solution.py:300
  (15 shorter events, 0.1 us)
Async XLA Ops:
  0.7 0.7 copy-start.5
  1.4 1.0 copy-start
  2.4 0.8 copy-start.2
  4.4 18.2 %copy-start.4 = (bf16[1,1024,384]{2,1,0:T(8,128)(2,1)S(1)}, bf16[1,1024,384]{2,1,0:T(8,128)(2,1)}, u32[]{:S(2)}) copy-start(bf16[1,1024,384]{2,1,0:T(8,128)(2,1)} %param.9) | copy-start | bytes 2359300
  4.4 73.0 %all-to-all-start = ((bf16[8,40,1024]{2,1,0:T(8,128)(2,1)}), bf16[8,40,1024]{2,1,0:T(8,128)(2,1)S(1)}, u32[]{:S(2)}, u32[]{:S(2)}) async-start(bf16[8,40,1024]{2,1,0:T(8,128)(2,1)} %shard_map.73), calls=%async_computation | async-start | bytes 1310720 | tf_op jit(solution)/shard_map/all_to_all | solution.py:257
  84.2 17.5 %collective-permute-start = (bf16[1024,256]{1,0:T(8,128)(2,1)S(1)}, bf16[1024,256]{1,0:T(8,128)(2,1)S(1)}, u32[]{:S(2)}, u32[]{:S(2)}) collective-permute-start(bf16[1024,256]{1,0:T(8,128)(2,1)S(1)} %get-tuple-element.49.half_ref.own_ref), channel_id=1, source_target_pairs={{0,1},{1,0},{2,3},{3,2},{4,5},{5,4},{6,7},{7,6},{8,9},{9,8},{10,11... | collective-permute-start | bytes 1572872 | tf_op jit(solution)/shard_map/ppermute | solution.py:37
  101.7 0.7 copy-start.3
  132.8 4.2 %copy-start.1 = (f32[384,256]{1,0:T(8,128)S(1)}, f32[384,256]{1,0:T(8,128)}, u32[]{:S(2)}) copy-start(f32[384,256]{1,0:T(8,128)} %first_ref.1) | copy-start | bytes 1179652
  132.8 15.5 %all-to-all-start.2 = ((f32[16,40,256]{2,1,0:T(8,128)}), f32[16,40,256]{2,1,0:T(8,128)S(1)}, u32[]{:S(2)}, u32[]{:S(2)}) async-start(f32[16,40,256]{2,1,0:T(8,128)} %broadcast_in_dim.37), calls=%async_computation.2 | async-start | bytes 1310720 | tf_op jit(solution)/shard_map/all_to_all | solution.py:33
  137.0 0.7 copy-start.6

commit v4 on v2

v4 whole, which is shorter than its diff:
```python
import jax
import jax.numpy as jnp
from jax import lax
from jax.experimental import pallas as pl
from jax.experimental.pallas import tpu as pltpu
from jax.sharding import Mesh
from jax.sharding import PartitionSpec as P

SLOTS = 31
GROUP = 8
PANEL = 128
ROW = ("z", "xh")
HIGHEST = lax.Precision.HIGHEST
F32 = jnp.float32
BF16 = jnp.bfloat16
LIMIT = pltpu.CompilerParams(vmem_limit_bytes=48 * 1024 * 1024)


def iota(shape, dim):
    return lax.broadcasted_iota(jnp.int32, shape, dim)


def contract(a, b, dim_a, dim_b, precision=None):
    return lax.dot_general(
        a, b, (((dim_a,), (dim_b,)), ((), ())), precision=precision, preferred_element_type=F32
    )


def swapped(x):
    return lax.ppermute(x, "xh", [(0, 1), (1, 0)])


def my_row():
    return lax.axis_index("z") * 2 + lax.axis_index("xh")


def places(panel_row, rows_pair, holders):
    win = panel_row.shape[1]
    holder = jnp.zeros_like(panel_row)
    for z in range(1, holders):
        holder = holder + (panel_row >= z * rows_pair).astype(jnp.int32)
    across = jnp.broadcast_to(holder, (win, win))
    earlier, later = iota((win, win), 0), iota((win, win), 1)
    down = jnp.sum(jnp.where(earlier == later, across, 0), axis=1, keepdims=True)
    same = (across == down) & (earlier < later)
    rank = jnp.sum(same.astype(jnp.int32), axis=0, keepdims=True)
    return holder, rank


def pick_kernel(
    turn_ref, panel_ref, border_ref, barrier_ref, first_ref, picked_ref, put_ref, rounds_ref
):
    rows_inv, rows_dev = border_ref.shape
    win = panel_ref.shape[1]
    z_count = put_ref.shape[0]
    panel_row = panel_ref[...]
    holder, rank = places(panel_row, 2 * rows_dev, z_count)
    rounds_ref[0] = jnp.max(rank) + 1
    place = rank - turn_ref[0] * SLOTS
    local = panel_row - my_row() * rows_dev
    in_slot = place == iota((SLOTS, win), 0)
    mine = in_slot & (local >= 0) & (local < rows_dev)
    source = jnp.sum(jnp.where(mine, local + 1, 0), axis=1, keepdims=True) - 1
    pick = (source == iota((SLOTS, rows_dev), 1)).astype(F32).astype(BF16)
    picked = contract(pick, border_ref[...], 1, 1)
    for z in range(z_count):
        put_ref[z] = jnp.where(in_slot & (holder == z), 1.0, 0.0).astype(BF16)
    share = win // lax.axis_size("scen")
    at = lax.axis_index("scen") * share + iota((share, win), 0)
    on_diagonal = at == iota((share, win), 1)
    own = jnp.sum(jnp.where(on_diagonal, local, 0), axis=1, keepdims=True)
    hit = own == iota((share, rows_dev), 1)
    base = contract(hit.astype(F32), first_ref[...], 1, 0, HIGHEST)
    term = jnp.sum(jnp.where(hit, barrier_ref[...], 0.0), axis=1, keepdims=True)
    base = base + jnp.where(on_diagonal, term, 0.0)
    rounded = base.astype(BF16).astype(F32)
    fold = rows_inv // win
    step = share // fold
    lanes = [
        jnp.concatenate([part[step * i : step * (i + 1)] for i in range(fold)], axis=1)
        for part in (rounded, base - rounded)
    ]
    picked_ref[...] = jnp.concatenate([*lanes, picked], axis=0).astype(BF16)


def gather_round(turn, panel_row, border, barrier_row, first_section):
    rows_inv, rows_dev = border.shape
    win = panel_row.shape[1]
    z_count = lax.axis_size("z")
    lines = SLOTS + 2 * win // lax.axis_size("scen") * win // rows_inv
    vmem = pl.BlockSpec(memory_space=pltpu.VMEM)
    smem = pl.BlockSpec(memory_space=pltpu.SMEM)
    picked, put, most = pl.pallas_call(
        pick_kernel,
        out_shape=(
            jax.ShapeDtypeStruct((lines, rows_inv), BF16),
            jax.ShapeDtypeStruct((z_count, SLOTS, win), BF16),
            jax.ShapeDtypeStruct((1,), jnp.int32),
        ),
        in_specs=[smem, vmem, vmem, vmem, vmem],
        out_specs=(vmem, vmem, smem),
        compiler_params=LIMIT,
    )(turn, panel_row, border, barrier_row, first_section)
    both = lax.all_gather(picked, "xh", axis=0)
    pair = both[0] + both[1]
    everyone = lax.all_gather(pair[-SLOTS:], "z", axis=0)
    columns = lax.dot_general(
        everyone, put, (((0, 1), (0, 1)), ((), ())), preferred_element_type=F32
    ).astype(BF16)
    return columns, most[0], pair[:-SLOTS]


def solve_kernel(own_ref, other_ref, columns_ref, extra_ref, out_ref):
    extra, rows_inv = extra_ref.shape
    win = columns_ref.shape[1]
    xh = lax.axis_index("xh")
    columns = columns_ref[...]
    own = contract(own_ref[...], columns, 1, 0)
    other = contract(other_ref[...], columns, 1, 0)
    low = jnp.where(xh == 0, own, other)
    high = jnp.where(xh == 0, other, own)
    parts = extra_ref[...].astype(F32)
    fold = rows_inv // win
    step = extra // 2
    lanes = [
        parts[step * p : step * (p + 1), win * i : win * (i + 1)] for p in range(2) for i in range(fold)
    ]
    out_ref[...] = jnp.concatenate([low, high, *lanes], axis=0).astype(BF16)


def term_kernel(columns_ref, border_ref, gathered_ref, prob_ref, slot_ref, out_ref, base_ref):
    z_count, lines, win = gathered_ref.shape
    rows_inv = border_ref.shape[0]
    scen_count, per_scen, _ = out_ref.shape
    share = win // scen_count
    step = rows_inv // z_count
    solved = gathered_ref[:, :step, :].reshape(rows_inv, win)
    match = iota(prob_ref.shape, 1) == slot_ref[...]
    weight = jnp.sum(jnp.where(match, prob_ref[...], 0.0), axis=1, keepdims=True)
    block = contract(columns_ref[...], solved, 0, 0) * weight
    out_ref[:, :share, :] = block.reshape(scen_count, share, win)
    term = contract(border_ref[...], solved, 0, 0) * weight
    out_ref[:, share:, :] = term.reshape(scen_count, per_scen - share, win)
    parts = jnp.sum(gathered_ref[:, step:, :].astype(F32), axis=0)
    base_ref[...] = parts[:share] + parts[share:]


def sum_kernel(shares_ref, base_ref, out_ref):
    share = base_ref.shape[0]
    total = jnp.sum(shares_ref[...], axis=0)
    total = jnp.concatenate([total[:share] + base_ref[...], total[share:]], axis=0)
    out_ref[...] = jnp.broadcast_to(total[None], out_ref.shape)


def inverse_factor(symmetric):
    size = symmetric.shape[0]
    count = size // GROUP
    work = [symmetric[GROUP * i : GROUP * (i + 1), :] for i in range(count)]
    lane, sub = iota((GROUP, size), 1), iota((GROUP, size), 0)
    result = []
    for group in range(count):
        low = group * GROUP
        block = work[group]
        inside = (lane >= low) & (lane < low + GROUP)
        lower = [[None] * GROUP for _ in range(GROUP)]
        scale = [None] * GROUP
        entry = [
            [jnp.broadcast_to(block[i : i + 1, low + j : low + j + 1], block.shape) for j in range(i + 1)]
            for i in range(GROUP)
        ]
        for j in range(GROUP):
            pivot = entry[j][j]
            for t in range(j):
                pivot = pivot - lower[j][t] * lower[j][t]
            scale[j] = lax.rsqrt(pivot)
            for i in range(j + 1, GROUP):
                value = entry[i][j]
                for t in range(j):
                    value = value - lower[i][t] * lower[j][t]
                lower[i][j] = value * scale[j]
        forward = []
        for i in range(GROUP):
            row = jnp.broadcast_to(block[i : i + 1, :], block.shape)
            row = jnp.where(inside, jnp.where(lane == low + i, 1.0, 0.0), row)
            for j in range(i):
                row = row - lower[i][j] * forward[j]
            forward.append(row * scale[i])
        done = forward[0]
        for i in range(1, GROUP):
            done = jnp.where(sub == i, forward[i], done)
        result.append(jnp.where(lane <= sub + low, done, 0.0))
        if group + 1 == count:
            break
        back = [None] * GROUP
        for i in reversed(range(GROUP)):
            row = forward[i]
            for j in range(i + 1, GROUP):
                row = row - lower[j][i] * back[j]
            back[i] = row * scale[i]
        for later in range(group + 1, count):
            old = work[later]
            new = jnp.where(inside, 0.0, old)
            for j in range(GROUP):
                new = new - old[:, low + j : low + j + 1] * back[j]
            work[later] = new
    return jnp.concatenate(result, axis=0)


def factor_kernel(gathered_ref, base_ref, out_ref):
    scen_count, per_scen, win = gathered_ref.shape
    share = win // scen_count
    diag = gathered_ref[:, :share, :].reshape(win, win)
    rows = gathered_ref[:, share:, :].reshape(base_ref.shape) + base_ref[...]

    def symmetric(i, j):
        one = diag[i : i + PANEL, j : j + PANEL]
        other = diag[j : j + PANEL, i : i + PANEL]
        return 0.5 * (one + other.T)

    first = inverse_factor(symmetric(0, 0))
    across = contract(symmetric(PANEL, 0), first, 1, 1, HIGHEST)
    second = inverse_factor(symmetric(PANEL, PANEL) - contract(across, across, 1, 1, HIGHEST))
    left = contract(rows[:, :PANEL], first, 1, 1, HIGHEST)
    right = rows[:, PANEL:] - contract(left, across, 1, 1, HIGHEST)
    out_ref[:, :PANEL] = left
    out_ref[:, PANEL:] = contract(right, second, 1, 1, HIGHEST)


def per_device(borders, kkt_inverse, first_section, barrier, panel_vars, probability, assignment):
    border, inverse_rows = borders[0], kkt_inverse[0]
    rows_inv, rows_dev = border.shape
    win = first_section.shape[1]
    scen_count = lax.axis_size("scen")
    share = win // scen_count
    panel_row, barrier_row = panel_vars[None, :], barrier[None, :]

    other_rows = swapped(inverse_rows)

    def turn(number):
        return gather_round(number[None], panel_row, border, barrier_row, first_section)

    columns, most, extra = turn(jnp.int32(0))
    _, columns = lax.while_loop(
        lambda state: state[0] * SLOTS < most,
        lambda state: (state[0] + 1, state[1] + turn(state[0])[0]),
        (jnp.int32(1), columns),
    )

    own_lines = 2 * inverse_rows.shape[0]
    message = pl.pallas_call(
        solve_kernel,
        out_shape=jax.ShapeDtypeStruct((own_lines + 2 * share, win), BF16),
        compiler_params=LIMIT,
    )(inverse_rows, other_rows, columns, extra)
    gathered = lax.all_gather(message, "z", axis=0)

    per_scen = share + rows_dev // scen_count
    terms, base = pl.pallas_call(
        term_kernel,
        out_shape=(
            jax.ShapeDtypeStruct((scen_count, per_scen, win), F32),
            jax.ShapeDtypeStruct((share, win), F32),
        ),
        compiler_params=LIMIT,
    )(columns, border, gathered, probability[None, :], assignment[None, :])
    shares = lax.all_to_all(terms, "scen", 0, 0, tiled=True)
    copies = pl.pallas_call(
        sum_kernel,
        out_shape=jax.ShapeDtypeStruct((scen_count, per_scen, win), F32),
        compiler_params=LIMIT,
    )(shares, base)
    everyone = lax.all_to_all(copies, "scen", 0, 0, tiled=True)

    hits = (
        jnp.arange(rows_dev, dtype=jnp.int32)[:, None] + my_row() * rows_dev == panel_vars[None, :]
    )
    rows_base = first_section + jnp.where(hits, barrier[:, None], 0.0)
    return pl.pallas_call(
        factor_kernel,
        out_shape=jax.ShapeDtypeStruct((rows_dev, win), F32),
        compiler_params=LIMIT,
    )(everyone, rows_base)


def solution(mesh):
    torus = Mesh(mesh.devices.reshape(mesh.shape["scen"], 16, 2), ("scen", "z", "xh"))
    return jax.shard_map(
        per_device,
        mesh=torus,
        in_specs=(
            P("scen", None, ROW),
            P("scen", ROW, None),
            P(ROW, None),
            P(ROW),
            P(),
            P(),
            P("scen"),
        ),
        out_specs=P(ROW, None),
        check_vma=False,
    )
```

time: 143 us -> 139 us (0.972)
  blocking collectives: 98.9 us -> 96.8 us
  starting transfers between devices: 11.6 us -> 9.51 us
    ppermute x2 -> x1, starting transfers between devices: 7.6 us -> 5.47 us  [swapped(): return lax.ppermute(x, 'xh', [(0, 1), (1, 0)])]
    all_gather x3, blocking collectives: 67 us -> 65.5 us  [the longest x1 35.3 us: gather_round(): everyone = lax.all_gather(pair[-SLOTS:], 'z', axis=0)]
    pallas_call x1 -> x2, Pallas kernels: 2.07 us -> 3.08 us  [the longest x1 2.17 us: gather_round(): pl.pallas_call(pick_kernel, out_shape=(jax.ShapeDtypeStruct((lines, rows_...]
  transfers between devices with their start and end apart: 3 -> 2, of which waited for: 1 -> 1; matrix products, arithmetic and copies ran while one was open for 0% -> 1% of each run, Pallas kernels for 2% -> 2%
where the time goes in v4:
time: 139 us
  blocking collectives  96.8 us (70%)
  Pallas kernels  16.7 us (12%)
  waiting for transfers between devices  10.5 us (8%)
  starting transfers between devices  9.51 us (7%)
  local copies, waits for them, and re-layouts  3.43 us (2%)
    all_gather x1, blocking collectives, gather_round(): everyone = lax.all_gather(pair[-SLOTS:], 'z', axis=0)  35.3 us
    all_to_all x1, blocking collectives, per_device(): shares = lax.all_to_all(terms, 'scen', 0, 0, tiled=True)  31.4 us
    all_gather x1, blocking collectives, per_device(): gathered = lax.all_gather(message, 'z', axis=0)  24.2 us
    pallas_call x1, Pallas kernels, per_device(): pl.pallas_call(factor_kernel, out_shape=jax.ShapeDtypeStruct((rows_dev, w...  12.8 us
    all_to_all x1, waiting for transfers between devices, per_device(): everyone = lax.all_to_all(copies, 'scen', 0, 0, tiled=True)  10.5 us
    all_gather x1, blocking collectives, gather_round(): both = lax.all_gather(picked, 'xh', axis=0)  5.91 us
    ppermute x1, starting transfers between devices, swapped(): return lax.ppermute(x, 'xh', [(0, 1), (1, 0)])  5.47 us
    all_to_all x1, starting transfers between devices, per_device(): everyone = lax.all_to_all(copies, 'scen', 0, 0, tiled=True)  4.04 us
  transfers between devices with their start and end apart: 2, of which 1 were waited for; matrix products, arithmetic and copies ran while one was open for 1% of the time, Pallas kernels for 2%

profile of v4, /device:TPU:1, one launch (start us, length us, event | category | flops | bytes accessed | tf_op | source)
XLA Modules:
  0.0 139.0 jit_solution(3293075094272423405)
XLA Ops:
  0.0 5.5 %collective-permute-start = (bf16[32,1024]{1,0:T(8,128)(2,1)}, bf16[32,1024]{1,0:T(8,128)(2,1)S(1)}, u32[]{:S(2)}, u32[]{:S(2)}) collective-permute-start(bf16[32,1024]{1,0:T(8,128)(2,1)} %bitcast.40), channel_id=1, source_target_pairs={{0,1},{1,0},{2,3},{3,2},{4,5},{5,4},{6,7},{7,6},{8,9},{9,8},{10,11... | collective-permute-start | bytes 196616 | tf_op jit(solution)/shard_map/ppermute | solution.py:30
  5.5 0.7 broadcast_in_dim.31.barrier_ref
  6.2 0.0 copy-start.4
  6.2 0.7 copy-done.4
  6.8 2.2 %shard_map.73 = (bf16[39,1024]{1,0:T(8,128)(2,1)S(1)}, bf16[16,31,256]{2,1,0:T(8,128)(2,1)S(1)}, s32[1]{0:T(128)}) custom-call(s32[1]{0:T(128)} %constant.6.clone.1.turn_ref, s32[1,256]{1,0:T(1,128)S(1)} %bitcast.45, bf16[1024,384]{1,0:T(8,128)(2,1)} %bitcast.43, f32[1,384]{1,0:T(1,128)S(1)} %broadcast_in_dim.31.barrier_ref, f32[384,256]{1,0:T(8,128)} %first_ref.1), custom_call_target="tpu_custom_call" | custom-call | tf_op jit(solution)/shard_map/pallas_call | solution.py:93
  9.0 5.9 %all-gather.4 = bf16[2,39,1024]{2,1,0:T(8,128)(2,1)S(1)} all-gather(bf16[1,39,1024]{2,1,0:T(8,128)(2,1)S(1)} %bitcast.39), channel_id=3, replica_groups=mesh['scen'=16,'z'=16,'xh'=2] {'xh'}, dimensions={0}, use_global_device_ids=true | all-gather | bytes 239616 | tf_op jit(solution)/shard_map/all_gather | solution.py:104
  15.0 35.3 %all_gather.28 = bf16[16,31,1024]{2,1,0:T(8,128)(2,1)S(1)} all-gather(bf16[1,31,1024]{2,1,0:T(8,128)(2,1)S(1)} %slice.45), channel_id=1, replica_groups=mesh['scen'=16,'z'=16,'xh'=2] {'z'}, dimensions={0}, use_global_device_ids=true | all-gather | bytes 1079296 | tf_op jit(solution)/shard_map/all_gather | solution.py:106
  50.3 0.5 fusion.2
  50.8 0.6 copy-done.2
  51.4 0.1 copy-done.3
  51.5 0.6 while.10
  52.8 0.0 collective-permute-done.other_ref
  52.8 0.0 copy-done
  52.8 0.3 shard_map.74
  53.1 24.2 %all-gather.2 = bf16[1536,256]{1,0:T(8,128)(2,1)S(1)} all-gather(bf16[96,256]{1,0:T(8,128)(2,1)S(1)} %shard_map.74), channel_id=4, replica_groups=mesh['scen'=16,'z'=16,'xh'=2] {'z'}, dimensions={0}, use_global_device_ids=true | all-gather | bytes 835584 | tf_op jit(solution)/shard_map/all_gather | solution.py:255
  77.3 0.7 copy-done.1
  78.0 0.6 shard_map.75
  78.5 31.4 %all_to_all.10.shares_ref = f32[16,40,256]{2,1,0:T(8,128)S(1)} all-to-all(f32[16,40,256]{2,1,0:T(8,128)S(1)} %get-tuple-element.54), channel_id=1, replica_groups=mesh['scen'=16,'z'=16,'xh'=2] {'scen'}, dimensions={0} | all-to-all | bytes 1310720 | tf_op jit(solution)/shard_map/all_to_all | solution.py:266
  109.9 0.9 shard_map.76
  110.8 4.0 %all-to-all-start.1 = ((f32[16,40,256]{2,1,0:T(8,128)}), f32[16,40,256]{2,1,0:T(8,128)S(1)}, u32[]{:S(2)}, u32[]{:S(2)}) async-start(f32[16,40,256]{2,1,0:T(8,128)} %shard_map.76), calls=%async_computation.1 | async-start | bytes 1310720 | tf_op jit(solution)/shard_map/all_to_all | solution.py:272
  114.9 0.7 copy-done.5
  115.5 0.2 select_add_fusion.base_ref
  115.7 10.5 %all-to-all-done.1.gathered_ref = f32[16,40,256]{2,1,0:T(8,128)S(1)} async-done(((f32[16,40,256]{2,1,0:T(8,128)}), f32[16,40,256]{2,1,0:T(8,128)S(1)}, u32[]{:S(2)}, u32[]{:S(2)}) %all-to-all-start.1) | async-done | bytes 655392 | tf_op jit(solution)/shard_map/all_to_all | solution.py:272
  126.2 12.8 %shard_map.77 = f32[384,256]{1,0:T(8,128)} custom-call(f32[16,40,256]{2,1,0:T(8,128)S(1)} %all-to-all-done.1.gathered_ref, f32[384,256]{1,0:T(8,128)S(1)} %select_add_fusion.base_ref), custom_call_target="tpu_custom_call" | custom-call | tf_op jit(solution)/shard_map/pallas_call | solution.py:278
  (9 shorter events, 0.0 us)
Async XLA Ops:
  0.0 52.8 %collective-permute-start = (bf16[32,1024]{1,0:T(8,128)(2,1)}, bf16[32,1024]{1,0:T(8,128)(2,1)S(1)}, u32[]{:S(2)}, u32[]{:S(2)}) collective-permute-start(bf16[32,1024]{1,0:T(8,128)(2,1)} %bitcast.40), channel_id=1, source_target_pairs={{0,1},{1,0},{2,3},{3,2},{4,5},{5,4},{6,7},{7,6},{8,9},{9,8},{10,11... | collective-permute-start | bytes 196616 | tf_op jit(solution)/shard_map/ppermute | solution.py:30
  6.2 0.7 copy-start.4
  50.3 1.1 copy-start.2
  50.3 1.2 copy-start.3
  51.5 1.3 copy-start
  77.3 0.7 copy-start.1
  110.8 15.4 %all-to-all-start.1 = ((f32[16,40,256]{2,1,0:T(8,128)}), f32[16,40,256]{2,1,0:T(8,128)S(1)}, u32[]{:S(2)}, u32[]{:S(2)}) async-start(f32[16,40,256]{2,1,0:T(8,128)} %shard_map.76), calls=%async_computation.1 | async-start | bytes 1310720 | tf_op jit(solution)/shard_map/all_to_all | solution.py:272
  114.9 0.7 copy-start.5

commit v5 on v4

--- a/solution.py
+++ b/solution.py
@@ -10,6 +10,7 @@
 GROUP = 8
 PANEL = 128
 ROW = ("z", "xh")
+SCEN = ("chip", "core")
 HIGHEST = lax.Precision.HIGHEST
 F32 = jnp.float32
 BF16 = jnp.bfloat16
@@ -65,8 +66,8 @@
     picked = contract(pick, border_ref[...], 1, 1)
     for z in range(z_count):
         put_ref[z] = jnp.where(in_slot & (holder == z), 1.0, 0.0).astype(BF16)
-    share = win // lax.axis_size("scen")
-    at = lax.axis_index("scen") * share + iota((share, win), 0)
+    share = win // lax.axis_size(SCEN)
+    at = lax.axis_index(SCEN) * share + iota((share, win), 0)
     on_diagonal = at == iota((share, win), 1)
     own = jnp.sum(jnp.where(on_diagonal, local, 0), axis=1, keepdims=True)
     hit = own == iota((share, rows_dev), 1)
@@ -87,7 +88,7 @@
     rows_inv, rows_dev = border.shape
     win = panel_row.shape[1]
     z_count = lax.axis_size("z")
-    lines = SLOTS + 2 * win // lax.axis_size("scen") * win // rows_inv
+    lines = SLOTS + 2 * win // lax.axis_size(SCEN) * win // rows_inv
     vmem = pl.BlockSpec(memory_space=pltpu.VMEM)
     smem = pl.BlockSpec(memory_space=pltpu.SMEM)
     picked, put, most = pl.pallas_call(
@@ -128,21 +129,32 @@
     out_ref[...] = jnp.concatenate([low, high, *lanes], axis=0).astype(BF16)
 
 
-def term_kernel(columns_ref, border_ref, gathered_ref, prob_ref, slot_ref, out_ref, base_ref):
+def term_kernel(
+    columns_ref, border_ref, gathered_ref, prob_ref, slot_ref, keep_ref, give_ref, base_ref
+):
     z_count, lines, win = gathered_ref.shape
     rows_inv = border_ref.shape[0]
-    scen_count, per_scen, _ = out_ref.shape
-    share = win // scen_count
+    chips, per_scen, _ = keep_ref.shape
+    share = base_ref.shape[0]
     step = rows_inv // z_count
     solved = gathered_ref[:, :step, :].reshape(rows_inv, win)
-    match = iota(prob_ref.shape, 1) == slot_ref[...]
-    weight = jnp.sum(jnp.where(match, prob_ref[...], 0.0), axis=1, keepdims=True)
+    weight = prob_ref[slot_ref[0]]
+    core = lax.axis_index("core")
     block = contract(columns_ref[...], solved, 0, 0) * weight
-    out_ref[:, :share, :] = block.reshape(scen_count, share, win)
+    block = block.reshape(chips, 2, share, win)
     term = contract(border_ref[...], solved, 0, 0) * weight
-    out_ref[:, share:, :] = term.reshape(scen_count, per_scen - share, win)
+    term = term.reshape(chips, 2, per_scen - share, win)
+    keep_ref[:, :share, :] = jnp.where(core == 0, block[:, 0], block[:, 1])
+    give_ref[:, :share, :] = jnp.where(core == 0, block[:, 1], block[:, 0])
+    keep_ref[:, share:, :] = jnp.where(core == 0, term[:, 0], term[:, 1])
+    give_ref[:, share:, :] = jnp.where(core == 0, term[:, 1], term[:, 0])
     parts = jnp.sum(gathered_ref[:, step:, :].astype(F32), axis=0)
     base_ref[...] = parts[:share] + parts[share:]
+
+
+def pair_kernel(keep_ref, given_ref, out_ref):
+    other = jnp.where(lax.axis_index("core") == 0, given_ref[1], given_ref[0])
+    out_ref[...] = keep_ref[...] + other
 
 
 def sum_kernel(shares_ref, base_ref, out_ref):
@@ -152,65 +164,77 @@
     out_ref[...] = jnp.broadcast_to(total[None], out_ref.shape)
 
 
+def tree_sum(terms):
+    while len(terms) > 1:
+        terms = [sum(terms[i : i + 2][1:], terms[i]) for i in range(0, len(terms), 2)]
+    return terms[0]
+
+
 def inverse_factor(symmetric):
     size = symmetric.shape[0]
     count = size // GROUP
+    shape = (GROUP, size)
     work = [symmetric[GROUP * i : GROUP * (i + 1), :] for i in range(count)]
-    lane, sub = iota((GROUP, size), 1), iota((GROUP, size), 0)
+    lane, sub = iota(shape, 1), iota(shape, 0)
     result = []
     for group in range(count):
         low = group * GROUP
         block = work[group]
         inside = (lane >= low) & (lane < low + GROUP)
-        lower = [[None] * GROUP for _ in range(GROUP)]
-        scale = [None] * GROUP
         entry = [
-            [jnp.broadcast_to(block[i : i + 1, low + j : low + j + 1], block.shape) for j in range(i + 1)]
+            [jnp.broadcast_to(block[i : i + 1, low + j : low + j + 1], shape) for j in range(i + 1)]
             for i in range(GROUP)
         ]
+        pivot = [None] * GROUP
+        lower = [[None] * GROUP for _ in range(GROUP)]
         for j in range(GROUP):
-            pivot = entry[j][j]
-            for t in range(j):
-                pivot = pivot - lower[j][t] * lower[j][t]
-            scale[j] = lax.rsqrt(pivot)
+            pivot[j] = 1.0 / entry[j][j]
             for i in range(j + 1, GROUP):
-                value = entry[i][j]
-                for t in range(j):
-                    value = value - lower[i][t] * lower[j][t]
-                lower[i][j] = value * scale[j]
-        forward = []
+                lower[i][j] = entry[i][j] * pivot[j]
+            for i in range(j + 1, GROUP):
+                for t in range(j + 1, i + 1):
+                    entry[i][t] = entry[i][t] - (entry[i][j] * entry[t][j]) * pivot[j]
+        unit = [[None] * GROUP for _ in range(GROUP)]
         for i in range(GROUP):
-            row = jnp.broadcast_to(block[i : i + 1, :], block.shape)
-            row = jnp.where(inside, jnp.where(lane == low + i, 1.0, 0.0), row)
             for j in range(i):
-                row = row - lower[i][j] * forward[j]
-            forward.append(row * scale[i])
-        done = forward[0]
+                value = lower[i][j]
+                for t in range(j + 1, i):
+                    value = value + lower[i][t] * unit[t][j]
+                unit[i][j] = -value
+        rows = jnp.where(inside, jnp.where(lane == sub + low, 1.0, 0.0), block)
+        terms = [rows]
+        for j in range(GROUP - 1):
+            column = jnp.zeros(shape, F32)
+            for i in range(j + 1, GROUP):
+                column = jnp.where(sub == i, unit[i][j], column)
+            terms.append(column * jnp.broadcast_to(rows[j : j + 1, :], shape))
+        forward = tree_sum(terms)
+        scale = pivot[0]
         for i in range(1, GROUP):
-            done = jnp.where(sub == i, forward[i], done)
-        result.append(jnp.where(lane <= sub + low, done, 0.0))
+            scale = jnp.where(sub == i, pivot[i], scale)
+        result.append(jnp.where(lane <= sub + low, forward * jnp.sqrt(scale), 0.0))
         if group + 1 == count:
             break
-        back = [None] * GROUP
-        for i in reversed(range(GROUP)):
-            row = forward[i]
-            for j in range(i + 1, GROUP):
-                row = row - lower[j][i] * back[j]
-            back[i] = row * scale[i]
+        scaled = forward * scale
+        scaled = [jnp.broadcast_to(scaled[i : i + 1, :], shape) for i in range(GROUP)]
+        back = [
+            tree_sum([scaled[j]] + [unit[i][j] * scaled[i] for i in range(j + 1, GROUP)])
+            for j in range(GROUP)
+        ]
         for later in range(group + 1, count):
             old = work[later]
-            new = jnp.where(inside, 0.0, old)
-            for j in range(GROUP):
-                new = new - old[:, low + j : low + j + 1] * back[j]
-            work[later] = new
+            taken = tree_sum([old[:, low + j : low + j + 1] * back[j] for j in range(GROUP)])
+            work[later] = jnp.where(inside, 0.0, old) - taken
     return jnp.concatenate(result, axis=0)
 
 
 def factor_kernel(gathered_ref, base_ref, out_ref):
-    scen_count, per_scen, win = gathered_ref.shape
-    share = win // scen_count
-    diag = gathered_ref[:, :share, :].reshape(win, win)
-    rows = gathered_ref[:, share:, :].reshape(base_ref.shape) + base_ref[...]
+    cores, chips, per_scen, win = gathered_ref.shape
+    share = win // (cores * chips)
+    order = [(core, chip) for chip in range(chips) for core in range(cores)]
+    diag = jnp.concatenate([gathered_ref[core, chip, :share, :] for core, chip in order], axis=0)
+    rows = jnp.concatenate([gathered_ref[core, chip, share:, :] for core, chip in order], axis=0)
+    rows = rows + base_ref[...]
 
     def symmetric(i, j):
         one = diag[i : i + PANEL, j : j + PANEL]
@@ -230,7 +254,7 @@
     border, inverse_rows = borders[0], kkt_inverse[0]
     rows_inv, rows_dev = border.shape
     win = first_section.shape[1]
-    scen_count = lax.axis_size("scen")
+    scen_count = lax.axis_size(SCEN)
     share = win // scen_count
     panel_row, barrier_row = panel_vars[None, :], barrier[None, :]
 
@@ -255,21 +279,21 @@
     gathered = lax.all_gather(message, "z", axis=0)
 
     per_scen = share + rows_dev // scen_count
-    terms, base = pl.pallas_call(
+    vmem = pl.BlockSpec(memory_space=pltpu.VMEM)
+    smem = pl.BlockSpec(memory_space=pltpu.SMEM)
+    half = jax.ShapeDtypeStruct((lax.axis_size("chip"), per_scen, win), F32)
+    keep, give, base = pl.pallas_call(
         term_kernel,
-        out_shape=(
-            jax.ShapeDtypeStruct((scen_count, per_scen, win), F32),
-            jax.ShapeDtypeStruct((share, win), F32),
-        ),
+        out_shape=(half, half, jax.ShapeDtypeStruct((share, win), F32)),
+        in_specs=[vmem, vmem, vmem, smem, smem],
         compiler_params=LIMIT,
-    )(columns, border, gathered, probability[None, :], assignment[None, :])
-    shares = lax.all_to_all(terms, "scen", 0, 0, tiled=True)
-    copies = pl.pallas_call(
-        sum_kernel,
-        out_shape=jax.ShapeDtypeStruct((scen_count, per_scen, win), F32),
-        compiler_params=LIMIT,
-    )(shares, base)
-    everyone = lax.all_to_all(copies, "scen", 0, 0, tiled=True)
+    )(columns, border, gathered, probability, assignment)
+    given = lax.all_gather(give, "core", axis=0)
+    pair = pl.pallas_call(pair_kernel, out_shape=half, compiler_params=LIMIT)(keep, given)
+    shares = lax.all_to_all(pair, "chip", 0, 0, tiled=True)
+    copies = pl.pallas_call(sum_kernel, out_shape=half, compiler_params=LIMIT)(shares, base)
+    everyone = lax.all_to_all(copies, "chip", 0, 0, tiled=True)
+    everyone = lax.all_gather(everyone, "core", axis=0)
 
     hits = (
         jnp.arange(rows_dev, dtype=jnp.int32)[:, None] + my_row() * rows_dev == panel_vars[None, :]
@@ -283,18 +307,18 @@
 
 
 def solution(mesh):
-    torus = Mesh(mesh.devices.reshape(mesh.shape["scen"], 16, 2), ("scen", "z", "xh"))
+    torus = Mesh(mesh.devices.reshape(8, 2, 16, 2), (*SCEN, *ROW))
     return jax.shard_map(
         per_device,
         mesh=torus,
         in_specs=(
-            P("scen", None, ROW),
-            P("scen", ROW, None),
+            P(SCEN, None, ROW),
+            P(SCEN, ROW, None),
             P(ROW, None),
             P(ROW),
             P(),
             P(),
-            P("scen"),
+            P(SCEN),
         ),
         out_specs=P(ROW, None),
         check_vma=False,

time: 139 us -> 136 us (0.978)
  blocking collectives: 96.8 us -> 87.2 us
  starting transfers between devices: 9.51 us -> 13.1 us
  waiting for transfers between devices: 10.5 us -> 13 us
    all_to_all x1 -> x0, blocking collectives: 31.4 us -> none  [per_device(): shares = lax.all_to_all(terms, 'scen', 0, 0, tiled=True)]
    all_gather x0 -> x2, blocking collectives: none -> 21.7 us  [the longest x1 17.2 us: per_device(): given = lax.all_gather(give, 'core', axis=0)]
    all_to_all x1 -> x2, starting transfers between devices: 4.04 us -> 7.65 us  [the longest x1 4.22 us: per_device(): shares = lax.all_to_all(pair, 'chip', 0, 0, tiled=True)]
    all_to_all x1 -> x2, waiting for transfers between devices: 10.5 us -> 13 us  [the longest x1 7.4 us: per_device(): shares = lax.all_to_all(pair, 'chip', 0, 0, tiled=True)]
  transfers between devices with their start and end apart: 2 -> 3, of which waited for: 1 -> 2; matrix products, arithmetic and copies ran while one was open for 1% -> 1% of each run, Pallas kernels for 2% -> 2%
where the time goes in v5:
time: 136 us; the launch traced here: 135 us
  blocking collectives  87.2 us (64%)
  Pallas kernels  16.5 us (12%)
  starting transfers between devices  13.1 us (10%)
  waiting for transfers between devices  13 us (10%)
  local copies, waits for them, and re-layouts  3.44 us (3%)
    all_gather x1, blocking collectives, gather_round(): everyone = lax.all_gather(pair[-SLOTS:], 'z', axis=0)  35.3 us
    all_gather x1, blocking collectives, per_device(): gathered = lax.all_gather(message, 'z', axis=0)  24.2 us
    all_gather x1, blocking collectives, per_device(): given = lax.all_gather(give, 'core', axis=0)  17.2 us
    pallas_call x1, Pallas kernels, per_device(): pl.pallas_call(factor_kernel, out_shape=jax.ShapeDtypeStruct((rows_dev, w...  11.4 us
    all_to_all x1, waiting for transfers between devices, per_device(): shares = lax.all_to_all(pair, 'chip', 0, 0, tiled=True)  7.4 us
    all_gather x1, blocking collectives, gather_round(): both = lax.all_gather(picked, 'xh', axis=0)  5.91 us
    all_to_all x1, waiting for transfers between devices, per_device(): everyone = lax.all_to_all(copies, 'chip', 0, 0, tiled=True)  5.61 us
    ppermute x1, starting transfers between devices, swapped(): return lax.ppermute(x, 'xh', [(0, 1), (1, 0)])  5.47 us
  transfers between devices with their start and end apart: 3, of which 2 were waited for; matrix products, arithmetic and copies ran while one was open for 1% of the time, Pallas kernels for 2%

profile of v5, /device:TPU:1, one launch (start us, length us, event | category | flops | bytes accessed | tf_op | source)
XLA Modules:
  0.0 135.3 jit_solution(12894877220965148378)
XLA Ops:
  0.0 5.5 %collective-permute-start = (bf16[32,1024]{1,0:T(8,128)(2,1)}, bf16[32,1024]{1,0:T(8,128)(2,1)S(1)}, u32[]{:S(2)}, u32[]{:S(2)}) collective-permute-start(bf16[32,1024]{1,0:T(8,128)(2,1)} %bitcast.41), channel_id=1, source_target_pairs={{0,1},{1,0},{2,3},{3,2},{4,5},{5,4},{6,7},{7,6},{8,9},{9,8},{10,11... | collective-permute-start | bytes 196616 | tf_op jit(solution)/shard_map/ppermute | solution.py:31
  5.5 0.7 broadcast_in_dim.25.barrier_ref
  6.2 0.7 copy-done.4
  6.8 2.2 %shard_map.73 = (bf16[39,1024]{1,0:T(8,128)(2,1)S(1)}, bf16[16,31,256]{2,1,0:T(8,128)(2,1)S(1)}, s32[1]{0:T(128)}) custom-call(s32[1]{0:T(128)} %constant.6.clone.1.turn_ref, s32[1,256]{1,0:T(1,128)S(1)} %bitcast.45, bf16[1024,384]{1,0:T(8,128)(2,1)} %bitcast.43, f32[1,384]{1,0:T(1,128)S(1)} %broadcast_in_dim.25.barrier_ref, f32[384,256]{1,0:T(8,128)} %first_ref.1), custom_call_target="tpu_custom_call" | custom-call | tf_op jit(solution)/shard_map/pallas_call | solution.py:94
  9.0 5.9 %all-gather.6 = bf16[2,39,1024]{2,1,0:T(8,128)(2,1)S(1)} all-gather(bf16[1,39,1024]{2,1,0:T(8,128)(2,1)S(1)} %bitcast.40), channel_id=3, replica_groups=mesh['chip'=8,'core'=2,'z'=16,'xh'=2] {'xh'}, dimensions={0}, use_global_device_ids=true | all-gather | bytes 239616 | tf_op jit(solution)/shard_map/all_gather | solution.py:105
  15.0 35.3 %all_gather.40 = bf16[16,31,1024]{2,1,0:T(8,128)(2,1)S(1)} all-gather(bf16[1,31,1024]{2,1,0:T(8,128)(2,1)S(1)} %slice.45), channel_id=1, replica_groups=mesh['chip'=8,'core'=2,'z'=16,'xh'=2] {'z'}, dimensions={0}, use_global_device_ids=true | all-gather | bytes 1079296 | tf_op jit(solution)/shard_map/all_gather | solution.py:107
  50.3 0.5 fusion.2
  50.8 0.6 copy-done.2
  51.5 0.7 while.10
  52.9 0.3 shard_map.74
  53.1 24.2 %all-gather.2 = bf16[1536,256]{1,0:T(8,128)(2,1)S(1)} all-gather(bf16[96,256]{1,0:T(8,128)(2,1)S(1)} %shard_map.74), channel_id=4, replica_groups=mesh['chip'=8,'core'=2,'z'=16,'xh'=2] {'z'}, dimensions={0}, use_global_device_ids=true | all-gather | bytes 835584 | tf_op jit(solution)/shard_map/all_gather | solution.py:279
  77.3 0.7 copy-done.1
  78.0 1.1 shard_map.75
  79.1 17.2 %all-gather.3 = f32[16,40,256]{2,1,0:T(8,128)S(1)} all-gather(f32[8,40,256]{2,1,0:T(8,128)S(1)} %get-tuple-element.56), channel_id=5, replica_groups=mesh['chip'=8,'core'=2,'z'=16,'xh'=2] {'core'}, dimensions={0}, use_global_device_ids=true | all-gather | bytes 983040 | tf_op jit(solution)/shard_map/all_gather | solution.py:291
  96.3 0.8 shard_map.76
  97.1 4.2 %all-to-all-start = ((f32[8,40,256]{2,1,0:T(8,128)}), f32[8,40,256]{2,1,0:T(8,128)S(1)}, u32[]{:S(2)}, u32[]{:S(2)}) async-start(f32[8,40,256]{2,1,0:T(8,128)} %shard_map.76), calls=%async_computation | async-start | bytes 655360 | tf_op jit(solution)/shard_map/all_to_all | solution.py:293
  101.3 7.4 %all-to-all-done.shares_ref = f32[8,40,256]{2,1,0:T(8,128)S(1)} async-done(((f32[8,40,256]{2,1,0:T(8,128)}), f32[8,40,256]{2,1,0:T(8,128)S(1)}, u32[]{:S(2)}, u32[]{:S(2)}) %all-to-all-start) | async-done | bytes 327712 | tf_op jit(solution)/shard_map/all_to_all | solution.py:293
  108.7 0.8 shard_map.77
  109.5 3.4 %all-to-all-start.1 = ((f32[8,40,256]{2,1,0:T(8,128)}), f32[8,40,256]{2,1,0:T(8,128)S(1)}, u32[]{:S(2)}, u32[]{:S(2)}) async-start(f32[8,40,256]{2,1,0:T(8,128)} %shard_map.77), calls=%async_computation.1 | async-start | bytes 655360 | tf_op jit(solution)/shard_map/all_to_all | solution.py:295
  112.9 0.7 copy-done.5
  113.6 0.2 select_add_fusion.base_ref
  113.8 5.6 %all-to-all-done.1 = f32[8,40,256]{2,1,0:T(8,128)S(1)} async-done(((f32[8,40,256]{2,1,0:T(8,128)}), f32[8,40,256]{2,1,0:T(8,128)S(1)}, u32[]{:S(2)}, u32[]{:S(2)}) %all-to-all-start.1) | async-done | bytes 327712 | tf_op jit(solution)/shard_map/all_to_all | solution.py:295
  119.4 4.5 %all-gather.4 = f32[16,40,256]{2,1,0:T(8,128)S(1)} all-gather(f32[8,40,256]{2,1,0:T(8,128)S(1)} %all-to-all-done.1), channel_id=6, replica_groups=mesh['chip'=8,'core'=2,'z'=16,'xh'=2] {'core'}, dimensions={0}, use_global_device_ids=true | all-gather | bytes 983040 | tf_op jit(solution)/shard_map/all_gather | solution.py:296
  123.9 11.4 %shard_map.78 = f32[384,256]{1,0:T(8,128)} custom-call(f32[2,8,40,256]{3,2,1,0:T(8,128)S(1)} %bitcast.38, f32[384,256]{1,0:T(8,128)S(1)} %select_add_fusion.base_ref), custom_call_target="tpu_custom_call" | custom-call | tf_op jit(solution)/shard_map/pallas_call | solution.py:302
  (13 shorter events, 0.1 us)
Async XLA Ops:
  0.0 52.8 %collective-permute-start = (bf16[32,1024]{1,0:T(8,128)(2,1)}, bf16[32,1024]{1,0:T(8,128)(2,1)S(1)}, u32[]{:S(2)}, u32[]{:S(2)}) collective-permute-start(bf16[32,1024]{1,0:T(8,128)(2,1)} %bitcast.41), channel_id=1, source_target_pairs={{0,1},{1,0},{2,3},{3,2},{4,5},{5,4},{6,7},{7,6},{8,9},{9,8},{10,11... | collective-permute-start | bytes 196616 | tf_op jit(solution)/shard_map/ppermute | solution.py:31
  6.2 0.7 copy-start.4
  50.3 1.1 copy-start.2
  50.3 1.2 copy-start.3
  51.5 1.3 copy-start
  77.3 0.7 copy-start.1
  97.1 11.6 %all-to-all-start = ((f32[8,40,256]{2,1,0:T(8,128)}), f32[8,40,256]{2,1,0:T(8,128)S(1)}, u32[]{:S(2)}, u32[]{:S(2)}) async-start(f32[8,40,256]{2,1,0:T(8,128)} %shard_map.76), calls=%async_computation | async-start | bytes 655360 | tf_op jit(solution)/shard_map/all_to_all | solution.py:293
  109.5 9.9 %all-to-all-start.1 = ((f32[8,40,256]{2,1,0:T(8,128)}), f32[8,40,256]{2,1,0:T(8,128)S(1)}, u32[]{:S(2)}, u32[]{:S(2)}) async-start(f32[8,40,256]{2,1,0:T(8,128)} %shard_map.77), calls=%async_computation.1 | async-start | bytes 655360 | tf_op jit(solution)/shard_map/all_to_all | solution.py:295
  112.9 0.7 copy-start.5

commit v6 on v5

--- a/solution.py
+++ b/solution.py
@@ -25,10 +25,6 @@
     return lax.dot_general(
         a, b, (((dim_a,), (dim_b,)), ((), ())), precision=precision, preferred_element_type=F32
     )
-
-
-def swapped(x):
-    return lax.ppermute(x, "xh", [(0, 1), (1, 0)])
 
 
 def my_row():
@@ -49,12 +45,24 @@
 
 
 def pick_kernel(
-    turn_ref, panel_ref, border_ref, barrier_ref, first_ref, picked_ref, put_ref, rounds_ref
+    turn_ref,
+    prob_ref,
+    slot_ref,
+    panel_ref,
+    border_ref,
+    inverse_ref,
+    barrier_ref,
+    first_ref,
+    message_ref,
+    put_ref,
+    weight_ref,
+    rounds_ref,
 ):
     rows_inv, rows_dev = border_ref.shape
-    win = panel_ref.shape[1]
+    win = first_ref.shape[1]
     z_count = put_ref.shape[0]
-    panel_row = panel_ref[...]
+    weight_ref[...] = jnp.full(weight_ref.shape, prob_ref[slot_ref[0]], F32)
+    panel_row = panel_ref[...][None, :]
     holder, rank = places(panel_row, 2 * rows_dev, z_count)
     rounds_ref[0] = jnp.max(rank) + 1
     place = rank - turn_ref[0] * SLOTS
@@ -72,7 +80,7 @@
     own = jnp.sum(jnp.where(on_diagonal, local, 0), axis=1, keepdims=True)
     hit = own == iota((share, rows_dev), 1)
     base = contract(hit.astype(F32), first_ref[...], 1, 0, HIGHEST)
-    term = jnp.sum(jnp.where(hit, barrier_ref[...], 0.0), axis=1, keepdims=True)
+    term = jnp.sum(jnp.where(hit, barrier_ref[...][None, :], 0.0), axis=1, keepdims=True)
     base = base + jnp.where(on_diagonal, term, 0.0)
     rounded = base.astype(BF16).astype(F32)
     fold = rows_inv // win
@@ -81,80 +89,82 @@
         jnp.concatenate([part[step * i : step * (i + 1)] for i in range(fold)], axis=1)
         for part in (rounded, base - rounded)
     ]
-    picked_ref[...] = jnp.concatenate([*lanes, picked], axis=0).astype(BF16)
-
-
-def gather_round(turn, panel_row, border, barrier_row, first_section):
+    lines = [*lanes, inverse_ref[...].astype(F32), picked]
+    message_ref[...] = jnp.concatenate(lines, axis=0).astype(BF16)
+
+
+def gather_round(turn, border, inverse_rows, first_section, barrier, panel_vars, prob, slot):
     rows_inv, rows_dev = border.shape
-    win = panel_row.shape[1]
+    win = panel_vars.shape[0]
     z_count = lax.axis_size("z")
-    lines = SLOTS + 2 * win // lax.axis_size(SCEN) * win // rows_inv
+    extra = 2 * win // lax.axis_size(SCEN) * win // rows_inv
     vmem = pl.BlockSpec(memory_space=pltpu.VMEM)
     smem = pl.BlockSpec(memory_space=pltpu.SMEM)
-    picked, put, most = pl.pallas_call(
+    message, put, weight, most = pl.pallas_call(
         pick_kernel,
         out_shape=(
-            jax.ShapeDtypeStruct((lines, rows_inv), BF16),
+            jax.ShapeDtypeStruct((extra + inverse_rows.shape[0] + SLOTS, rows_inv), BF16),
             jax.ShapeDtypeStruct((z_count, SLOTS, win), BF16),
+            jax.ShapeDtypeStruct((1, win), F32),
             jax.ShapeDtypeStruct((1,), jnp.int32),
         ),
-        in_specs=[smem, vmem, vmem, vmem, vmem],
-        out_specs=(vmem, vmem, smem),
+        in_specs=[smem, smem, smem, vmem, vmem, vmem, vmem, vmem],
+        out_specs=(vmem, vmem, vmem, smem),
         compiler_params=LIMIT,
-    )(turn, panel_row, border, barrier_row, first_section)
-    both = lax.all_gather(picked, "xh", axis=0)
-    pair = both[0] + both[1]
-    everyone = lax.all_gather(pair[-SLOTS:], "z", axis=0)
+    )(turn, prob, slot, panel_vars, border, inverse_rows, barrier, first_section)
+    both = lax.all_gather(message, "xh", axis=0)
+    mine = both[0, -SLOTS:] + both[1, -SLOTS:]
+    everyone = lax.all_gather(mine, "z", axis=0)
     columns = lax.dot_general(
         everyone, put, (((0, 1), (0, 1)), ((), ())), preferred_element_type=F32
     ).astype(BF16)
-    return columns, most[0], pair[:-SLOTS]
-
-
-def solve_kernel(own_ref, other_ref, columns_ref, extra_ref, out_ref):
-    extra, rows_inv = extra_ref.shape
+    return columns, most[0], both[:, :-SLOTS], weight
+
+
+def solve_kernel(both_ref, columns_ref, out_ref):
+    _, lines, rows_inv = both_ref.shape
     win = columns_ref.shape[1]
-    xh = lax.axis_index("xh")
-    columns = columns_ref[...]
-    own = contract(own_ref[...], columns, 1, 0)
-    other = contract(other_ref[...], columns, 1, 0)
-    low = jnp.where(xh == 0, own, other)
-    high = jnp.where(xh == 0, other, own)
-    parts = extra_ref[...].astype(F32)
+    own = rows_inv // (2 * lax.axis_size("z"))
+    extra = lines - own
+    both = both_ref[...].astype(F32)
+    rows = both[:, extra:, :].reshape(2 * own, rows_inv).astype(BF16)
+    solved = contract(rows, columns_ref[...], 1, 0)
+    parts = both[0, :extra, :] + both[1, :extra, :]
     fold = rows_inv // win
     step = extra // 2
     lanes = [
         parts[step * p : step * (p + 1), win * i : win * (i + 1)] for p in range(2) for i in range(fold)
     ]
-    out_ref[...] = jnp.concatenate([low, high, *lanes], axis=0).astype(BF16)
-
-
-def term_kernel(
-    columns_ref, border_ref, gathered_ref, prob_ref, slot_ref, keep_ref, give_ref, base_ref
-):
+    out_ref[...] = jnp.concatenate([solved, *lanes], axis=0).astype(BF16)
+
+
+def term_kernel(columns_ref, border_ref, gathered_ref, weight_ref, keep_ref, give_ref, base_ref):
     z_count, lines, win = gathered_ref.shape
     rows_inv = border_ref.shape[0]
     chips, per_scen, _ = keep_ref.shape
     share = base_ref.shape[0]
     step = rows_inv // z_count
     solved = gathered_ref[:, :step, :].reshape(rows_inv, win)
-    weight = prob_ref[slot_ref[0]]
-    core = lax.axis_index("core")
+    weight = weight_ref[...]
     block = contract(columns_ref[...], solved, 0, 0) * weight
     block = block.reshape(chips, 2, share, win)
     term = contract(border_ref[...], solved, 0, 0) * weight
     term = term.reshape(chips, 2, per_scen - share, win)
-    keep_ref[:, :share, :] = jnp.where(core == 0, block[:, 0], block[:, 1])
-    give_ref[:, :share, :] = jnp.where(core == 0, block[:, 1], block[:, 0])
-    keep_ref[:, share:, :] = jnp.where(core == 0, term[:, 0], term[:, 1])
-    give_ref[:, share:, :] = jnp.where(core == 0, term[:, 1], term[:, 0])
+    for core in range(2):
+
+        @pl.when(lax.axis_index("core") == core)
+        def _(core=core):
+            keep_ref[:, :share, :] = block[:, core]
+            keep_ref[:, share:, :] = term[:, core]
+            give_ref[:, :share, :] = block[:, 1 - core]
+            give_ref[:, share:, :] = term[:, 1 - core]
+
     parts = jnp.sum(gathered_ref[:, step:, :].astype(F32), axis=0)
     base_ref[...] = parts[:share] + parts[share:]
 
 
 def pair_kernel(keep_ref, given_ref, out_ref):
-    other = jnp.where(lax.axis_index("core") == 0, given_ref[1], given_ref[0])
-    out_ref[...] = keep_ref[...] + other
+    out_ref[...] = keep_ref[...] + given_ref[1 - lax.axis_index("core")]
 
 
 def sum_kernel(shares_ref, base_ref, out_ref):
@@ -256,14 +266,20 @@
     win = first_section.shape[1]
     scen_count = lax.axis_size(SCEN)
     share = win // scen_count
-    panel_row, barrier_row = panel_vars[None, :], barrier[None, :]
-
-    other_rows = swapped(inverse_rows)
 
     def turn(number):
-        return gather_round(number[None], panel_row, border, barrier_row, first_section)
-
-    columns, most, extra = turn(jnp.int32(0))
+        return gather_round(
+            number[None],
+            border,
+            inverse_rows,
+            first_section,
+            barrier,
+            panel_vars,
+            probability,
+            assignment,
+        )
+
+    columns, most, both, weight = turn(jnp.int32(0))
     _, columns = lax.while_loop(
         lambda state: state[0] * SLOTS < most,
         lambda state: (state[0] + 1, state[1] + turn(state[0])[0]),
@@ -275,19 +291,16 @@
         solve_kernel,
         out_shape=jax.ShapeDtypeStruct((own_lines + 2 * share, win), BF16),
         compiler_params=LIMIT,
-    )(inverse_rows, other_rows, columns, extra)
+    )(both, columns)
     gathered = lax.all_gather(message, "z", axis=0)
 
     per_scen = share + rows_dev // scen_count
-    vmem = pl.BlockSpec(memory_space=pltpu.VMEM)
-    smem = pl.BlockSpec(memory_space=pltpu.SMEM)
     half = jax.ShapeDtypeStruct((lax.axis_size("chip"), per_scen, win), F32)
     keep, give, base = pl.pallas_call(
         term_kernel,
         out_shape=(half, half, jax.ShapeDtypeStruct((share, win), F32)),
-        in_specs=[vmem, vmem, vmem, smem, smem],
         compiler_params=LIMIT,
-    )(columns, border, gathered, probability, assignment)
+    )(columns, border, gathered, weight)
     given = lax.all_gather(give, "core", axis=0)
     pair = pl.pallas_call(pair_kernel, out_shape=half, compiler_params=LIMIT)(keep, given)
     shares = lax.all_to_all(pair, "chip", 0, 0, tiled=True)

time: 136 us -> 131 us (0.963)
  starting transfers between devices: 13.1 us -> 8.55 us
  local copies, waits for them, and re-layouts: 3.44 us -> 1.42 us
  blocking collectives: 87.2 us -> 89 us
    ppermute x1 -> x0, starting transfers between devices: 5.47 us -> none  [swapped(): return lax.ppermute(x, 'xh', [(0, 1), (1, 0)])]
    all_gather x2, blocking collectives: 41.2 us -> 43.2 us  [the longest x1 36.5 us: gather_round(): everyone = lax.all_gather(mine, 'z', axis=0)]
  transfers between devices with their start and end apart: 3 -> 2, of which waited for: 2 -> 2; matrix products, arithmetic and copies ran while one was open for 1% -> 0% of each run, Pallas kernels for 2% -> 0%
where the time goes in v6:
time: 131 us
  blocking collectives  89 us (68%)
  Pallas kernels  16 us (12%)
  waiting for transfers between devices  13.7 us (10%)
  starting transfers between devices  8.55 us (7%)
  local copies, waits for them, and re-layouts  1.42 us (1%)
    all_gather x1, blocking collectives, gather_round(): everyone = lax.all_gather(mine, 'z', axis=0)  36.5 us
    all_gather x1, blocking collectives, per_device(): gathered = lax.all_gather(message, 'z', axis=0)  24.2 us
    all_gather x1, blocking collectives, per_device(): given = lax.all_gather(give, 'core', axis=0)  17 us
    pallas_call x1, Pallas kernels, per_device(): pl.pallas_call(factor_kernel, out_shape=jax.ShapeDtypeStruct((rows_dev, w...  11.4 us
    all_to_all x1, waiting for transfers between devices, per_device(): shares = lax.all_to_all(pair, 'chip', 0, 0, tiled=True)  7.4 us
    all_gather x1, blocking collectives, gather_round(): both = lax.all_gather(message, 'xh', axis=0)  6.76 us
    all_to_all x1, waiting for transfers between devices, per_device(): everyone = lax.all_to_all(copies, 'chip', 0, 0, tiled=True)  6.28 us
    all_to_all x1, starting transfers between devices, per_device(): shares = lax.all_to_all(pair, 'chip', 0, 0, tiled=True)  5.12 us
  transfers between devices with their start and end apart: 2, of which 2 were waited for; matrix products, arithmetic and copies ran while one was open for 0% of the time, Pallas kernels for 0%

profile of v6, /device:TPU:1, one launch (start us, length us, event | category | flops | bytes accessed | tf_op | source)
XLA Modules:
  0.0 130.6 jit_solution(3214439798444682575)
XLA Ops:
  0.7 0.0 copy-start.3
  0.7 0.7 copy-done.3
  1.3 0.0 copy-done.4
  1.3 0.0 copy-done.5
  1.4 2.2 %shard_map.73 = (bf16[71,1024]{1,0:T(8,128)(2,1)S(1)}, bf16[16,31,256]{2,1,0:T(8,128)(2,1)S(1)}, f32[1,256]{1,0:T(1,128)S(1)}, s32[1]{0:T(128)}) custom-call(s32[1]{0:T(128)} %constant.6.clone.1.turn_ref, f32[16]{0:T(128)S(1)} %copy-done.5, s32[1]{0:T(128)S(6)} %copy.14.slot_ref, s32[256]{0:T(256)S(1)} %copy-done.4, bf16[1024,384]{1,0:T(8,128)(2,1)} %bitcast.38, ...), custom_call_target="tpu_custom_call" | custom-call | tf_op jit(solution)/shard_map/pallas_call | solution.py:103
  3.6 6.8 %all-gather.6 = bf16[2,71,1024]{2,1,0:T(8,128)(2,1)S(1)} all-gather(bf16[1,71,1024]{2,1,0:T(8,128)(2,1)S(1)} %bitcast.37), channel_id=3, replica_groups=mesh['chip'=8,'core'=2,'z'=16,'xh'=2] {'xh'}, dimensions={0}, use_global_device_ids=true | all-gather | bytes 436224 | tf_op jit(solution)/shard_map/all_gather | solution.py:115
  10.4 36.5 %all_gather.40 = bf16[16,31,1024]{2,1,0:T(8,128)(2,1)S(1)} all-gather(bf16[1,31,1024]{2,1,0:T(8,128)(2,1)S(1)} %slice_add_fusion.1), channel_id=1, replica_groups=mesh['chip'=8,'core'=2,'z'=16,'xh'=2] {'z'}, dimensions={0}, use_global_device_ids=true | all-gather | bytes 1079296 | tf_op jit(solution)/shard_map/all_gather | solution.py:117
  46.9 0.5 fusion.2
  47.4 0.6 copy-done
  48.0 0.1 copy-done.1
  48.1 0.6 while.10
  48.7 0.2 shard_map.74
  48.9 24.2 %all-gather.2 = bf16[1536,256]{1,0:T(8,128)(2,1)S(1)} all-gather(bf16[96,256]{1,0:T(8,128)(2,1)S(1)} %shard_map.74), channel_id=4, replica_groups=mesh['chip'=8,'core'=2,'z'=16,'xh'=2] {'z'}, dimensions={0}, use_global_device_ids=true | all-gather | bytes 835584 | tf_op jit(solution)/shard_map/all_gather | solution.py:295
  73.1 0.6 shard_map.75
  73.7 17.0 %all-gather.3 = f32[16,40,256]{2,1,0:T(8,128)S(1)} all-gather(f32[8,40,256]{2,1,0:T(8,128)S(1)} %get-tuple-element.73), channel_id=5, replica_groups=mesh['chip'=8,'core'=2,'z'=16,'xh'=2] {'core'}, dimensions={0}, use_global_device_ids=true | all-gather | bytes 983040 | tf_op jit(solution)/shard_map/all_gather | solution.py:304
  90.7 0.8 shard_map.76
  91.5 5.1 %all-to-all-start = ((f32[8,40,256]{2,1,0:T(8,128)}), f32[8,40,256]{2,1,0:T(8,128)S(1)}, u32[]{:S(2)}, u32[]{:S(2)}) async-start(f32[8,40,256]{2,1,0:T(8,128)} %shard_map.76), calls=%async_computation | async-start | bytes 655360 | tf_op jit(solution)/shard_map/all_to_all | solution.py:306
  96.6 7.4 %all-to-all-done.shares_ref = f32[8,40,256]{2,1,0:T(8,128)S(1)} async-done(((f32[8,40,256]{2,1,0:T(8,128)}), f32[8,40,256]{2,1,0:T(8,128)S(1)}, u32[]{:S(2)}, u32[]{:S(2)}) %all-to-all-start) | async-done | bytes 327712 | tf_op jit(solution)/shard_map/all_to_all | solution.py:306
  104.0 0.8 shard_map.77
  104.8 3.4 %all-to-all-start.1 = ((f32[8,40,256]{2,1,0:T(8,128)}), f32[8,40,256]{2,1,0:T(8,128)S(1)}, u32[]{:S(2)}, u32[]{:S(2)}) async-start(f32[8,40,256]{2,1,0:T(8,128)} %shard_map.77), calls=%async_computation.1 | async-start | bytes 655360 | tf_op jit(solution)/shard_map/all_to_all | solution.py:308
  108.2 0.2 select_add_fusion.base_ref
  108.4 6.3 %all-to-all-done.1 = f32[8,40,256]{2,1,0:T(8,128)S(1)} async-done(((f32[8,40,256]{2,1,0:T(8,128)}), f32[8,40,256]{2,1,0:T(8,128)S(1)}, u32[]{:S(2)}, u32[]{:S(2)}) %all-to-all-start.1) | async-done | bytes 327712 | tf_op jit(solution)/shard_map/all_to_all | solution.py:308
  114.7 4.5 %all-gather.4 = f32[16,40,256]{2,1,0:T(8,128)S(1)} all-gather(f32[8,40,256]{2,1,0:T(8,128)S(1)} %all-to-all-done.1), channel_id=6, replica_groups=mesh['chip'=8,'core'=2,'z'=16,'xh'=2] {'core'}, dimensions={0}, use_global_device_ids=true | all-gather | bytes 983040 | tf_op jit(solution)/shard_map/all_gather | solution.py:309
  119.2 11.4 %shard_map.78 = f32[384,256]{1,0:T(8,128)} custom-call(f32[2,8,40,256]{3,2,1,0:T(8,128)S(1)} %bitcast.36, f32[384,256]{1,0:T(8,128)S(1)} %select_add_fusion.base_ref), custom_call_target="tpu_custom_call" | custom-call | tf_op jit(solution)/shard_map/pallas_call | solution.py:315
  (9 shorter events, 0.0 us)
Async XLA Ops:
  0.7 0.7 copy-start.3
  0.7 0.7 copy-start.4
  0.7 0.7 copy-start.5
  46.9 1.1 copy-start
  46.9 1.2 copy-start.1
  46.9 1.2 copy-start.2
  91.5 12.5 %all-to-all-start = ((f32[8,40,256]{2,1,0:T(8,128)}), f32[8,40,256]{2,1,0:T(8,128)S(1)}, u32[]{:S(2)}, u32[]{:S(2)}) async-start(f32[8,40,256]{2,1,0:T(8,128)} %shard_map.76), calls=%async_computation | async-start | bytes 655360 | tf_op jit(solution)/shard_map/all_to_all | solution.py:306
  104.8 9.9 %all-to-all-start.1 = ((f32[8,40,256]{2,1,0:T(8,128)}), f32[8,40,256]{2,1,0:T(8,128)S(1)}, u32[]{:S(2)}, u32[]{:S(2)}) async-start(f32[8,40,256]{2,1,0:T(8,128)} %shard_map.77), calls=%async_computation.1 | async-start | bytes 655360 | tf_op jit(solution)/shard_map/all_to_all | solution.py:308

commit v7 on v6

--- a/solution.py
+++ b/solution.py
@@ -161,17 +161,6 @@
 
     parts = jnp.sum(gathered_ref[:, step:, :].astype(F32), axis=0)
     base_ref[...] = parts[:share] + parts[share:]
-
-
-def pair_kernel(keep_ref, given_ref, out_ref):
-    out_ref[...] = keep_ref[...] + given_ref[1 - lax.axis_index("core")]
-
-
-def sum_kernel(shares_ref, base_ref, out_ref):
-    share = base_ref.shape[0]
-    total = jnp.sum(shares_ref[...], axis=0)
-    total = jnp.concatenate([total[:share] + base_ref[...], total[share:]], axis=0)
-    out_ref[...] = jnp.broadcast_to(total[None], out_ref.shape)
 
 
 def tree_sum(terms):
@@ -231,10 +220,23 @@
             tree_sum([scaled[j]] + [unit[i][j] * scaled[i] for i in range(j + 1, GROUP)])
             for j in range(GROUP)
         ]
-        for later in range(group + 1, count):
+        near = group + 2 if count - group > 4 else count
+        for later in range(group + 1, near):
             old = work[later]
             taken = tree_sum([old[:, low + j : low + j + 1] * back[j] for j in range(GROUP)])
             work[later] = jnp.where(inside, 0.0, old) - taken
+        if near < count:
+            stacked = back[0]
+            for j in range(1, GROUP):
+                stacked = jnp.where(sub == j, back[j], stacked)
+            zero = jnp.zeros(shape, F32)
+            spread = [stacked if i == group else zero for i in range(count)]
+            taken = contract(
+                jnp.concatenate(work[near:], axis=0), jnp.concatenate(spread, axis=0), 1, 0, HIGHEST
+            )
+            for later in range(near, count):
+                at = GROUP * (later - near)
+                work[later] = jnp.where(inside, 0.0, work[later]) - taken[at : at + GROUP]
     return jnp.concatenate(result, axis=0)
 
 
@@ -302,9 +304,10 @@
         compiler_params=LIMIT,
     )(columns, border, gathered, weight)
     given = lax.all_gather(give, "core", axis=0)
-    pair = pl.pallas_call(pair_kernel, out_shape=half, compiler_params=LIMIT)(keep, given)
+    pair = keep + lax.dynamic_index_in_dim(given, 1 - lax.axis_index("core"), 0, keepdims=False)
     shares = lax.all_to_all(pair, "chip", 0, 0, tiled=True)
-    copies = pl.pallas_call(sum_kernel, out_shape=half, compiler_params=LIMIT)(shares, base)
+    total = jnp.sum(shares, axis=0) + jnp.pad(base, ((0, per_scen - share), (0, 0)))
+    copies = jnp.broadcast_to(total[None], half.shape)
     everyone = lax.all_to_all(copies, "chip", 0, 0, tiled=True)
     everyone = lax.all_gather(everyone, "core", axis=0)
 

time: 131 us -> 130 us (level)
  Pallas kernels: 16 us -> 12.9 us
    pallas_call x1, Pallas kernels: 11.4 us -> 9.81 us  [per_device(): pl.pallas_call(factor_kernel, out_shape=jax.ShapeDtypeStruct((rows_dev, w...]
    pallas_call x2 -> x0, Pallas kernels: 1.52 us -> none  [the longest x1 0.76 us: per_device(): pl.pallas_call(pair_kernel, out_shape=half, compiler_params=LIMIT)]
where the time goes in v7:
time: 130 us; the launch traced here: 129 us
  blocking collectives  89 us (68%)
  waiting for transfers between devices  13.7 us (11%)
  Pallas kernels  12.9 us (10%)
  starting transfers between devices  8.55 us (7%)
  local copies, waits for them, and re-layouts  2.17 us (2%)
    all_gather x1, blocking collectives, gather_round(): everyone = lax.all_gather(mine, 'z', axis=0)  36.5 us
    all_gather x1, blocking collectives, per_device(): gathered = lax.all_gather(message, 'z', axis=0)  24.2 us
    all_gather x1, blocking collectives, per_device(): given = lax.all_gather(give, 'core', axis=0)  17 us
    pallas_call x1, Pallas kernels, per_device(): pl.pallas_call(factor_kernel, out_shape=jax.ShapeDtypeStruct((rows_dev, w...  9.81 us
    all_to_all x1, waiting for transfers between devices, per_device(): shares = lax.all_to_all(pair, 'chip', 0, 0, tiled=True)  7.4 us
    all_gather x1, blocking collectives, gather_round(): both = lax.all_gather(message, 'xh', axis=0)  6.76 us
    all_to_all x1, waiting for transfers between devices, per_device(): everyone = lax.all_to_all(copies, 'chip', 0, 0, tiled=True)  6.28 us
    all_to_all x1, starting transfers between devices, per_device(): shares = lax.all_to_all(pair, 'chip', 0, 0, tiled=True)  5.12 us
  transfers between devices with their start and end apart: 2, of which 2 were waited for; matrix products, arithmetic and copies ran while one was open for 0% of the time, Pallas kernels for 0%

profile of v7, /device:TPU:1, one launch (start us, length us, event | category | flops | bytes accessed | tf_op | source)
XLA Modules:
  0.0 129.1 jit_solution(14570570667696969198)
XLA Ops:
  0.7 0.0 copy-start.3
  0.7 0.7 copy-done.3
  1.3 0.0 copy-done.4
  1.3 0.0 copy-done.5
  1.4 2.2 %shard_map.73 = (bf16[71,1024]{1,0:T(8,128)(2,1)S(1)}, bf16[16,31,256]{2,1,0:T(8,128)(2,1)S(1)}, f32[1,256]{1,0:T(1,128)S(1)}, s32[1]{0:T(128)}) custom-call(s32[1]{0:T(128)} %constant.15.clone.1.turn_ref, f32[16]{0:T(128)S(1)} %copy-done.5, s32[1]{0:T(128)S(6)} %copy.14.slot_ref, s32[256]{0:T(256)S(1)} %copy-done.4, bf16[1024,384]{1,0:T(8,128)(2,1)} %bitcast.39, ...), custom_call_target="tpu_custom_call" | custom-call | tf_op jit(solution)/shard_map/pallas_call | solution.py:103
  3.6 6.8 %all-gather.6 = bf16[2,71,1024]{2,1,0:T(8,128)(2,1)S(1)} all-gather(bf16[1,71,1024]{2,1,0:T(8,128)(2,1)S(1)} %bitcast.38), channel_id=3, replica_groups=mesh['chip'=8,'core'=2,'z'=16,'xh'=2] {'xh'}, dimensions={0}, use_global_device_ids=true | all-gather | bytes 436224 | tf_op jit(solution)/shard_map/all_gather | solution.py:115
  10.4 36.5 %all_gather.40 = bf16[16,31,1024]{2,1,0:T(8,128)(2,1)S(1)} all-gather(bf16[1,31,1024]{2,1,0:T(8,128)(2,1)S(1)} %slice_add_fusion.1), channel_id=1, replica_groups=mesh['chip'=8,'core'=2,'z'=16,'xh'=2] {'z'}, dimensions={0}, use_global_device_ids=true | all-gather | bytes 1079296 | tf_op jit(solution)/shard_map/all_gather | solution.py:117
  46.9 0.5 fusion.2
  47.4 0.6 copy-done
  48.0 0.1 copy-done.1
  48.1 0.6 while.10
  48.7 0.2 shard_map.74
  48.9 24.2 %all-gather.2 = bf16[1536,256]{1,0:T(8,128)(2,1)S(1)} all-gather(bf16[96,256]{1,0:T(8,128)(2,1)S(1)} %shard_map.74), channel_id=4, replica_groups=mesh['chip'=8,'core'=2,'z'=16,'xh'=2] {'z'}, dimensions={0}, use_global_device_ids=true | all-gather | bytes 835584 | tf_op jit(solution)/shard_map/all_gather | solution.py:297
  73.2 0.6 shard_map.75
  73.8 17.0 %all-gather.3 = f32[16,40,256]{2,1,0:T(8,128)S(1)} all-gather(f32[8,40,256]{2,1,0:T(8,128)S(1)} %get-tuple-element.73), channel_id=5, replica_groups=mesh['chip'=8,'core'=2,'z'=16,'xh'=2] {'core'}, dimensions={0}, use_global_device_ids=true | all-gather | bytes 983040 | tf_op jit(solution)/shard_map/all_gather | solution.py:306
  90.8 0.8 bitcast_add_fusion
  91.6 5.1 %all-to-all-start = ((f32[8,40,256]{2,1,0:T(8,128)}), f32[8,40,256]{2,1,0:T(8,128)S(1)}, u32[]{:S(2)}, u32[]{:S(2)}) async-start(f32[8,40,256]{2,1,0:T(8,128)} %bitcast_add_fusion), calls=%async_computation | async-start | bytes 655360 | tf_op jit(solution)/shard_map/all_to_all | solution.py:308
  96.7 7.4 %all-to-all-done = f32[8,40,256]{2,1,0:T(8,128)S(1)} async-done(((f32[8,40,256]{2,1,0:T(8,128)}), f32[8,40,256]{2,1,0:T(8,128)S(1)}, u32[]{:S(2)}, u32[]{:S(2)}) %all-to-all-start) | async-done | bytes 327712 | tf_op jit(solution)/shard_map/all_to_all | solution.py:308
  104.2 0.7 broadcast_in_dim.24
  104.9 3.4 %all-to-all-start.1 = ((f32[8,40,256]{2,1,0:T(8,128)}), f32[8,40,256]{2,1,0:T(8,128)S(1)}, u32[]{:S(2)}, u32[]{:S(2)}) async-start(f32[8,40,256]{2,1,0:T(8,128)} %broadcast_in_dim.24), calls=%async_computation.1 | async-start | bytes 655360 | tf_op jit(solution)/shard_map/all_to_all | solution.py:311
  108.4 0.2 select_add_fusion.base_ref
  108.5 6.3 %all-to-all-done.1 = f32[8,40,256]{2,1,0:T(8,128)S(1)} async-done(((f32[8,40,256]{2,1,0:T(8,128)}), f32[8,40,256]{2,1,0:T(8,128)S(1)}, u32[]{:S(2)}, u32[]{:S(2)}) %all-to-all-start.1) | async-done | bytes 327712 | tf_op jit(solution)/shard_map/all_to_all | solution.py:311
  114.8 4.5 %all-gather.4 = f32[16,40,256]{2,1,0:T(8,128)S(1)} all-gather(f32[8,40,256]{2,1,0:T(8,128)S(1)} %all-to-all-done.1), channel_id=6, replica_groups=mesh['chip'=8,'core'=2,'z'=16,'xh'=2] {'core'}, dimensions={0}, use_global_device_ids=true | all-gather | bytes 983040 | tf_op jit(solution)/shard_map/all_gather | solution.py:312
  119.3 9.8 %shard_map.76 = f32[384,256]{1,0:T(8,128)} custom-call(f32[2,8,40,256]{3,2,1,0:T(8,128)S(1)} %bitcast.37, f32[384,256]{1,0:T(8,128)S(1)} %select_add_fusion.base_ref), custom_call_target="tpu_custom_call" | custom-call | tf_op jit(solution)/shard_map/pallas_call | solution.py:318
  (11 shorter events, 0.1 us)
Async XLA Ops:
  0.7 0.7 copy-start.3
  0.7 0.7 copy-start.4
  0.7 0.7 copy-start.5
  46.9 1.1 copy-start
  46.9 1.2 copy-start.1
  46.9 1.2 copy-start.2
  91.6 12.5 %all-to-all-start = ((f32[8,40,256]{2,1,0:T(8,128)}), f32[8,40,256]{2,1,0:T(8,128)S(1)}, u32[]{:S(2)}, u32[]{:S(2)}) async-start(f32[8,40,256]{2,1,0:T(8,128)} %bitcast_add_fusion), calls=%async_computation | async-start | bytes 655360 | tf_op jit(solution)/shard_map/all_to_all | solution.py:308
  104.9 9.9 %all-to-all-start.1 = ((f32[8,40,256]{2,1,0:T(8,128)}), f32[8,40,256]{2,1,0:T(8,128)S(1)}, u32[]{:S(2)}, u32[]{:S(2)}) async-start(f32[8,40,256]{2,1,0:T(8,128)} %broadcast_in_dim.24), calls=%async_computation.1 | async-start | bytes 655360 | tf_op jit(solution)/shard_map/all_to_all | solution.py:311

commit v8 on v7

--- a/solution.py
+++ b/solution.py
@@ -25,6 +25,14 @@
     return lax.dot_general(
         a, b, (((dim_a,), (dim_b,)), ((), ())), precision=precision, preferred_element_type=F32
     )
+
+
+def contract_split(a, b, dim_a, dim_b):
+    a_high, b_high = a.astype(BF16), b.astype(BF16)
+    a_low = (a - a_high.astype(F32)).astype(BF16)
+    b_low = (b - b_high.astype(F32)).astype(BF16)
+    small = contract(a_high, b_low, dim_a, dim_b) + contract(a_low, b_high, dim_a, dim_b)
+    return contract(a_high, b_high, dim_a, dim_b) + small
 
 
 def my_row():
@@ -201,21 +209,18 @@
                     value = value + lower[i][t] * unit[t][j]
                 unit[i][j] = -value
         rows = jnp.where(inside, jnp.where(lane == sub + low, 1.0, 0.0), block)
-        terms = [rows]
-        for j in range(GROUP - 1):
-            column = jnp.zeros(shape, F32)
-            for i in range(j + 1, GROUP):
-                column = jnp.where(sub == i, unit[i][j], column)
-            terms.append(column * jnp.broadcast_to(rows[j : j + 1, :], shape))
-        forward = tree_sum(terms)
-        scale = pivot[0]
+        spots = [jnp.broadcast_to(rows[j : j + 1, :], shape) for j in range(GROUP)]
+        forward = [
+            tree_sum([spots[i]] + [unit[i][j] * spots[j] for j in range(i)]) for i in range(GROUP)
+        ]
+        done, scale = forward[0], pivot[0]
         for i in range(1, GROUP):
+            done = jnp.where(sub == i, forward[i], done)
             scale = jnp.where(sub == i, pivot[i], scale)
-        result.append(jnp.where(lane <= sub + low, forward * jnp.sqrt(scale), 0.0))
+        result.append(jnp.where(lane <= sub + low, done * jnp.sqrt(scale), 0.0))
         if group + 1 == count:
             break
-        scaled = forward * scale
-        scaled = [jnp.broadcast_to(scaled[i : i + 1, :], shape) for i in range(GROUP)]
+        scaled = [forward[i] * pivot[i] for i in range(GROUP)]
         back = [
             tree_sum([scaled[j]] + [unit[i][j] * scaled[i] for i in range(j + 1, GROUP)])
             for j in range(GROUP)
@@ -231,8 +236,8 @@
                 stacked = jnp.where(sub == j, back[j], stacked)
             zero = jnp.zeros(shape, F32)
             spread = [stacked if i == group else zero for i in range(count)]
-            taken = contract(
-                jnp.concatenate(work[near:], axis=0), jnp.concatenate(spread, axis=0), 1, 0, HIGHEST
+            taken = contract_split(
+                jnp.concatenate(work[near:], axis=0), jnp.concatenate(spread, axis=0), 1, 0
             )
             for later in range(near, count):
                 at = GROUP * (later - near)
@@ -254,12 +259,12 @@
         return 0.5 * (one + other.T)
 
     first = inverse_factor(symmetric(0, 0))
-    across = contract(symmetric(PANEL, 0), first, 1, 1, HIGHEST)
-    second = inverse_factor(symmetric(PANEL, PANEL) - contract(across, across, 1, 1, HIGHEST))
-    left = contract(rows[:, :PANEL], first, 1, 1, HIGHEST)
-    right = rows[:, PANEL:] - contract(left, across, 1, 1, HIGHEST)
+    across = contract_split(symmetric(PANEL, 0), first, 1, 1)
+    second = inverse_factor(symmetric(PANEL, PANEL) - contract_split(across, across, 1, 1))
+    left = contract_split(rows[:, :PANEL], first, 1, 1)
+    right = rows[:, PANEL:] - contract_split(left, across, 1, 1)
     out_ref[:, :PANEL] = left
-    out_ref[:, PANEL:] = contract(right, second, 1, 1, HIGHEST)
+    out_ref[:, PANEL:] = contract_split(right, second, 1, 1)
 
 
 def per_device(borders, kkt_inverse, first_section, barrier, panel_vars, probability, assignment):

time: 130 us -> 129 us (level)
  no operation moved by 1% of the time
where the time goes in v8:
time: 129 us; the launch traced here: 128 us
  blocking collectives  89 us (69%)
  waiting for transfers between devices  13.7 us (11%)
  Pallas kernels  11.9 us (9%)
  starting transfers between devices  8.55 us (7%)
  local copies, waits for them, and re-layouts  2.17 us (2%)
    all_gather x1, blocking collectives, gather_round(): everyone = lax.all_gather(mine, 'z', axis=0)  36.5 us
    all_gather x1, blocking collectives, per_device(): gathered = lax.all_gather(message, 'z', axis=0)  24.2 us
    all_gather x1, blocking collectives, per_device(): given = lax.all_gather(give, 'core', axis=0)  17 us
    pallas_call x1, Pallas kernels, per_device(): pl.pallas_call(factor_kernel, out_shape=jax.ShapeDtypeStruct((rows_dev, w...  8.9 us
    all_to_all x1, waiting for transfers between devices, per_device(): shares = lax.all_to_all(pair, 'chip', 0, 0, tiled=True)  7.4 us
    all_gather x1, blocking collectives, gather_round(): both = lax.all_gather(message, 'xh', axis=0)  6.76 us
    all_to_all x1, waiting for transfers between devices, per_device(): everyone = lax.all_to_all(copies, 'chip', 0, 0, tiled=True)  6.28 us
    all_to_all x1, starting transfers between devices, per_device(): shares = lax.all_to_all(pair, 'chip', 0, 0, tiled=True)  5.12 us
  transfers between devices with their start and end apart: 2, of which 2 were waited for; matrix products, arithmetic and copies ran while one was open for 0% of the time, Pallas kernels for 0%

profile of v8, /device:TPU:1, one launch (start us, length us, event | category | flops | bytes accessed | tf_op | source)
XLA Modules:
  0.0 128.2 jit_solution(10161431128283303215)
XLA Ops:
  0.7 0.0 copy-start.3
  0.7 0.0 copy-start.4
  0.7 0.7 copy-done.3
  1.3 0.0 copy-done.4
  1.4 2.2 %shard_map.73 = (bf16[71,1024]{1,0:T(8,128)(2,1)S(1)}, bf16[16,31,256]{2,1,0:T(8,128)(2,1)S(1)}, f32[1,256]{1,0:T(1,128)S(1)}, s32[1]{0:T(128)}) custom-call(s32[1]{0:T(128)} %constant.15.clone.1.turn_ref, f32[16]{0:T(128)S(1)} %copy-done.5, s32[1]{0:T(128)S(6)} %copy.14.slot_ref, s32[256]{0:T(256)S(1)} %copy-done.4, bf16[1024,384]{1,0:T(8,128)(2,1)} %bitcast.39, ...), custom_call_target="tpu_custom_call" | custom-call | tf_op jit(solution)/shard_map/pallas_call | solution.py:111
  3.6 6.8 %all-gather.6 = bf16[2,71,1024]{2,1,0:T(8,128)(2,1)S(1)} all-gather(bf16[1,71,1024]{2,1,0:T(8,128)(2,1)S(1)} %bitcast.38), channel_id=3, replica_groups=mesh['chip'=8,'core'=2,'z'=16,'xh'=2] {'xh'}, dimensions={0}, use_global_device_ids=true | all-gather | bytes 436224 | tf_op jit(solution)/shard_map/all_gather | solution.py:123
  10.4 36.5 %all_gather.40 = bf16[16,31,1024]{2,1,0:T(8,128)(2,1)S(1)} all-gather(bf16[1,31,1024]{2,1,0:T(8,128)(2,1)S(1)} %slice_add_fusion.1), channel_id=1, replica_groups=mesh['chip'=8,'core'=2,'z'=16,'xh'=2] {'z'}, dimensions={0}, use_global_device_ids=true | all-gather | bytes 1079296 | tf_op jit(solution)/shard_map/all_gather | solution.py:125
  46.9 0.5 fusion.2
  47.4 0.6 copy-done
  48.0 0.1 copy-done.1
  48.1 0.6 while.10
  48.7 0.2 shard_map.74
  48.9 24.2 %all-gather.2 = bf16[1536,256]{1,0:T(8,128)(2,1)S(1)} all-gather(bf16[96,256]{1,0:T(8,128)(2,1)S(1)} %shard_map.74), channel_id=4, replica_groups=mesh['chip'=8,'core'=2,'z'=16,'xh'=2] {'z'}, dimensions={0}, use_global_device_ids=true | all-gather | bytes 835584 | tf_op jit(solution)/shard_map/all_gather | solution.py:302
  73.2 0.6 shard_map.75
  73.8 17.0 %all-gather.3 = f32[16,40,256]{2,1,0:T(8,128)S(1)} all-gather(f32[8,40,256]{2,1,0:T(8,128)S(1)} %get-tuple-element.73), channel_id=5, replica_groups=mesh['chip'=8,'core'=2,'z'=16,'xh'=2] {'core'}, dimensions={0}, use_global_device_ids=true | all-gather | bytes 983040 | tf_op jit(solution)/shard_map/all_gather | solution.py:311
  90.8 0.8 bitcast_add_fusion
  91.6 5.1 %all-to-all-start = ((f32[8,40,256]{2,1,0:T(8,128)}), f32[8,40,256]{2,1,0:T(8,128)S(1)}, u32[]{:S(2)}, u32[]{:S(2)}) async-start(f32[8,40,256]{2,1,0:T(8,128)} %bitcast_add_fusion), calls=%async_computation | async-start | bytes 655360 | tf_op jit(solution)/shard_map/all_to_all | solution.py:313
  96.7 7.4 %all-to-all-done = f32[8,40,256]{2,1,0:T(8,128)S(1)} async-done(((f32[8,40,256]{2,1,0:T(8,128)}), f32[8,40,256]{2,1,0:T(8,128)S(1)}, u32[]{:S(2)}, u32[]{:S(2)}) %all-to-all-start) | async-done | bytes 327712 | tf_op jit(solution)/shard_map/all_to_all | solution.py:313
  104.2 0.7 broadcast_in_dim.24
  104.9 3.4 %all-to-all-start.1 = ((f32[8,40,256]{2,1,0:T(8,128)}), f32[8,40,256]{2,1,0:T(8,128)S(1)}, u32[]{:S(2)}, u32[]{:S(2)}) async-start(f32[8,40,256]{2,1,0:T(8,128)} %broadcast_in_dim.24), calls=%async_computation.1 | async-start | bytes 655360 | tf_op jit(solution)/shard_map/all_to_all | solution.py:316
  108.4 0.2 select_add_fusion.base_ref
  108.5 6.3 %all-to-all-done.1 = f32[8,40,256]{2,1,0:T(8,128)S(1)} async-done(((f32[8,40,256]{2,1,0:T(8,128)}), f32[8,40,256]{2,1,0:T(8,128)S(1)}, u32[]{:S(2)}, u32[]{:S(2)}) %all-to-all-start.1) | async-done | bytes 327712 | tf_op jit(solution)/shard_map/all_to_all | solution.py:316
  114.8 4.5 %all-gather.4 = f32[16,40,256]{2,1,0:T(8,128)S(1)} all-gather(f32[8,40,256]{2,1,0:T(8,128)S(1)} %all-to-all-done.1), channel_id=6, replica_groups=mesh['chip'=8,'core'=2,'z'=16,'xh'=2] {'core'}, dimensions={0}, use_global_device_ids=true | all-gather | bytes 983040 | tf_op jit(solution)/shard_map/all_gather | solution.py:317
  119.3 8.9 %shard_map.76 = f32[384,256]{1,0:T(8,128)} custom-call(f32[2,8,40,256]{3,2,1,0:T(8,128)S(1)} %bitcast.37, f32[384,256]{1,0:T(8,128)S(1)} %select_add_fusion.base_ref), custom_call_target="tpu_custom_call" | custom-call | tf_op jit(solution)/shard_map/pallas_call | solution.py:323
  (11 shorter events, 0.1 us)
Async XLA Ops:
  0.7 0.7 copy-start.3
  0.7 0.7 copy-start.4
  0.7 0.7 copy-start.5
  46.9 1.1 copy-start
  46.9 1.2 copy-start.1
  46.9 1.2 copy-start.2
  91.6 12.5 %all-to-all-start = ((f32[8,40,256]{2,1,0:T(8,128)}), f32[8,40,256]{2,1,0:T(8,128)S(1)}, u32[]{:S(2)}, u32[]{:S(2)}) async-start(f32[8,40,256]{2,1,0:T(8,128)} %bitcast_add_fusion), calls=%async_computation | async-start | bytes 655360 | tf_op jit(solution)/shard_map/all_to_all | solution.py:313
  104.9 9.9 %all-to-all-start.1 = ((f32[8,40,256]{2,1,0:T(8,128)}), f32[8,40,256]{2,1,0:T(8,128)S(1)}, u32[]{:S(2)}, u32[]{:S(2)}) async-start(f32[8,40,256]{2,1,0:T(8,128)} %broadcast_in_dim.24), calls=%async_computation.1 | async-start | bytes 655360 | tf_op jit(solution)/shard_map/all_to_all | solution.py:316

commit v9 on v8

--- a/solution.py
+++ b/solution.py
@@ -11,7 +11,6 @@
 PANEL = 128
 ROW = ("z", "xh")
 SCEN = ("chip", "core")
-HIGHEST = lax.Precision.HIGHEST
 F32 = jnp.float32
 BF16 = jnp.bfloat16
 LIMIT = pltpu.CompilerParams(vmem_limit_bytes=48 * 1024 * 1024)
@@ -21,10 +20,8 @@
     return lax.broadcasted_iota(jnp.int32, shape, dim)
 
 
-def contract(a, b, dim_a, dim_b, precision=None):
-    return lax.dot_general(
-        a, b, (((dim_a,), (dim_b,)), ((), ())), precision=precision, preferred_element_type=F32
-    )
+def contract(a, b, dim_a, dim_b):
+    return lax.dot_general(a, b, (((dim_a,), (dim_b,)), ((), ())), preferred_element_type=F32)
 
 
 def contract_split(a, b, dim_a, dim_b):
@@ -87,7 +84,11 @@
     on_diagonal = at == iota((share, win), 1)
     own = jnp.sum(jnp.where(on_diagonal, local, 0), axis=1, keepdims=True)
     hit = own == iota((share, rows_dev), 1)
-    base = contract(hit.astype(F32), first_ref[...], 1, 0, HIGHEST)
+    first = first_ref[...]
+    first_high = first.astype(BF16)
+    first_low = (first - first_high.astype(F32)).astype(BF16)
+    pick = hit.astype(F32).astype(BF16)
+    base = contract(pick, first_high, 1, 0) + contract(pick, first_low, 1, 0)
     term = jnp.sum(jnp.where(hit, barrier_ref[...][None, :], 0.0), axis=1, keepdims=True)
     base = base + jnp.where(on_diagonal, term, 0.0)
     rounded = base.astype(BF16).astype(F32)

time: 129 us -> 129 us (level)
  no operation moved by 1% of the time
where the time goes in v9:
time: 129 us; the launch traced here: 128 us
  blocking collectives  89 us (69%)
  waiting for transfers between devices  13.7 us (11%)
  Pallas kernels  12 us (9%)
  starting transfers between devices  8.55 us (7%)
  local copies, waits for them, and re-layouts  2.16 us (2%)
    all_gather x1, blocking collectives, gather_round(): everyone = lax.all_gather(mine, 'z', axis=0)  36.5 us
    all_gather x1, blocking collectives, per_device(): gathered = lax.all_gather(message, 'z', axis=0)  24.2 us
    all_gather x1, blocking collectives, per_device(): given = lax.all_gather(give, 'core', axis=0)  17 us
    pallas_call x1, Pallas kernels, per_device(): pl.pallas_call(factor_kernel, out_shape=jax.ShapeDtypeStruct((rows_dev, w...  8.9 us
    all_to_all x1, waiting for transfers between devices, per_device(): shares = lax.all_to_all(pair, 'chip', 0, 0, tiled=True)  7.4 us
    all_gather x1, blocking collectives, gather_round(): both = lax.all_gather(message, 'xh', axis=0)  6.76 us
    all_to_all x1, waiting for transfers between devices, per_device(): everyone = lax.all_to_all(copies, 'chip', 0, 0, tiled=True)  6.28 us
    all_to_all x1, starting transfers between devices, per_device(): shares = lax.all_to_all(pair, 'chip', 0, 0, tiled=True)  5.12 us
  transfers between devices with their start and end apart: 2, of which 2 were waited for; matrix products, arithmetic and copies ran while one was open for 0% of the time, Pallas kernels for 0%

profile of v9, /device:TPU:1, one launch (start us, length us, event | category | flops | bytes accessed | tf_op | source)
XLA Modules:
  0.0 128.2 jit_solution(14909793078877762740)
XLA Ops:
  0.7 0.0 copy-start.3
  0.7 0.7 copy-done.3
  1.3 0.0 copy-done.4
  1.3 0.0 copy-done.5
  1.4 2.2 %shard_map.73 = (bf16[71,1024]{1,0:T(8,128)(2,1)S(1)}, bf16[16,31,256]{2,1,0:T(8,128)(2,1)S(1)}, f32[1,256]{1,0:T(1,128)S(1)}, s32[1]{0:T(128)}) custom-call(s32[1]{0:T(128)} %constant.15.clone.1.turn_ref, f32[16]{0:T(128)S(1)} %copy-done.5, s32[1]{0:T(128)S(6)} %copy.14.slot_ref, s32[256]{0:T(256)S(1)} %copy-done.4, bf16[1024,384]{1,0:T(8,128)(2,1)} %bitcast.39, ...), custom_call_target="tpu_custom_call" | custom-call | tf_op jit(solution)/shard_map/pallas_call | solution.py:112
  3.6 6.8 %all-gather.6 = bf16[2,71,1024]{2,1,0:T(8,128)(2,1)S(1)} all-gather(bf16[1,71,1024]{2,1,0:T(8,128)(2,1)S(1)} %bitcast.38), channel_id=3, replica_groups=mesh['chip'=8,'core'=2,'z'=16,'xh'=2] {'xh'}, dimensions={0}, use_global_device_ids=true | all-gather | bytes 436224 | tf_op jit(solution)/shard_map/all_gather | solution.py:124
  10.4 36.5 %all_gather.40 = bf16[16,31,1024]{2,1,0:T(8,128)(2,1)S(1)} all-gather(bf16[1,31,1024]{2,1,0:T(8,128)(2,1)S(1)} %slice_add_fusion.1), channel_id=1, replica_groups=mesh['chip'=8,'core'=2,'z'=16,'xh'=2] {'z'}, dimensions={0}, use_global_device_ids=true | all-gather | bytes 1079296 | tf_op jit(solution)/shard_map/all_gather | solution.py:126
  46.9 0.5 fusion.2
  47.4 0.6 copy-done
  48.0 0.1 copy-done.1
  48.1 0.6 while.10
  48.7 0.2 shard_map.74
  49.0 24.2 %all-gather.2 = bf16[1536,256]{1,0:T(8,128)(2,1)S(1)} all-gather(bf16[96,256]{1,0:T(8,128)(2,1)S(1)} %shard_map.74), channel_id=4, replica_groups=mesh['chip'=8,'core'=2,'z'=16,'xh'=2] {'z'}, dimensions={0}, use_global_device_ids=true | all-gather | bytes 835584 | tf_op jit(solution)/shard_map/all_gather | solution.py:303
  73.2 0.6 shard_map.75
  73.8 17.0 %all-gather.3 = f32[16,40,256]{2,1,0:T(8,128)S(1)} all-gather(f32[8,40,256]{2,1,0:T(8,128)S(1)} %get-tuple-element.73), channel_id=5, replica_groups=mesh['chip'=8,'core'=2,'z'=16,'xh'=2] {'core'}, dimensions={0}, use_global_device_ids=true | all-gather | bytes 983040 | tf_op jit(solution)/shard_map/all_gather | solution.py:312
  90.8 0.8 bitcast_add_fusion
  91.6 5.1 %all-to-all-start = ((f32[8,40,256]{2,1,0:T(8,128)}), f32[8,40,256]{2,1,0:T(8,128)S(1)}, u32[]{:S(2)}, u32[]{:S(2)}) async-start(f32[8,40,256]{2,1,0:T(8,128)} %bitcast_add_fusion), calls=%async_computation | async-start | bytes 655360 | tf_op jit(solution)/shard_map/all_to_all | solution.py:314
  96.7 7.4 %all-to-all-done = f32[8,40,256]{2,1,0:T(8,128)S(1)} async-done(((f32[8,40,256]{2,1,0:T(8,128)}), f32[8,40,256]{2,1,0:T(8,128)S(1)}, u32[]{:S(2)}, u32[]{:S(2)}) %all-to-all-start) | async-done | bytes 327712 | tf_op jit(solution)/shard_map/all_to_all | solution.py:314
  104.2 0.7 broadcast_in_dim.24
  104.9 3.4 %all-to-all-start.1 = ((f32[8,40,256]{2,1,0:T(8,128)}), f32[8,40,256]{2,1,0:T(8,128)S(1)}, u32[]{:S(2)}, u32[]{:S(2)}) async-start(f32[8,40,256]{2,1,0:T(8,128)} %broadcast_in_dim.24), calls=%async_computation.1 | async-start | bytes 655360 | tf_op jit(solution)/shard_map/all_to_all | solution.py:317
  108.4 0.2 select_add_fusion.base_ref
  108.6 6.3 %all-to-all-done.1 = f32[8,40,256]{2,1,0:T(8,128)S(1)} async-done(((f32[8,40,256]{2,1,0:T(8,128)}), f32[8,40,256]{2,1,0:T(8,128)S(1)}, u32[]{:S(2)}, u32[]{:S(2)}) %all-to-all-start.1) | async-done | bytes 327712 | tf_op jit(solution)/shard_map/all_to_all | solution.py:317
  114.8 4.5 %all-gather.4 = f32[16,40,256]{2,1,0:T(8,128)S(1)} all-gather(f32[8,40,256]{2,1,0:T(8,128)S(1)} %all-to-all-done.1), channel_id=6, replica_groups=mesh['chip'=8,'core'=2,'z'=16,'xh'=2] {'core'}, dimensions={0}, use_global_device_ids=true | all-gather | bytes 983040 | tf_op jit(solution)/shard_map/all_gather | solution.py:318
  119.4 8.9 %shard_map.76 = f32[384,256]{1,0:T(8,128)} custom-call(f32[2,8,40,256]{3,2,1,0:T(8,128)S(1)} %bitcast.37, f32[384,256]{1,0:T(8,128)S(1)} %select_add_fusion.base_ref), custom_call_target="tpu_custom_call" | custom-call | tf_op jit(solution)/shard_map/pallas_call | solution.py:324
  (11 shorter events, 0.1 us)
Async XLA Ops:
  0.7 0.7 copy-start.3
  0.7 0.7 copy-start.4
  0.7 0.7 copy-start.5
  46.9 1.1 copy-start
  46.9 1.2 copy-start.1
  46.9 1.2 copy-start.2
  91.6 12.5 %all-to-all-start = ((f32[8,40,256]{2,1,0:T(8,128)}), f32[8,40,256]{2,1,0:T(8,128)S(1)}, u32[]{:S(2)}, u32[]{:S(2)}) async-start(f32[8,40,256]{2,1,0:T(8,128)} %bitcast_add_fusion), calls=%async_computation | async-start | bytes 655360 | tf_op jit(solution)/shard_map/all_to_all | solution.py:314
  104.9 9.9 %all-to-all-start.1 = ((f32[8,40,256]{2,1,0:T(8,128)}), f32[8,40,256]{2,1,0:T(8,128)S(1)}, u32[]{:S(2)}, u32[]{:S(2)}) async-start(f32[8,40,256]{2,1,0:T(8,128)} %broadcast_in_dim.24), calls=%async_computation.1 | async-start | bytes 655360 | tf_op jit(solution)/shard_map/all_to_all | solution.py:317

commit v10 on v9

--- a/solution.py
+++ b/solution.py
@@ -41,11 +41,11 @@
     holder = jnp.zeros_like(panel_row)
     for z in range(1, holders):
         holder = holder + (panel_row >= z * rows_pair).astype(jnp.int32)
-    across = jnp.broadcast_to(holder, (win, win))
+    across = jnp.broadcast_to(holder.astype(F32), (win, win))
     earlier, later = iota((win, win), 0), iota((win, win), 1)
-    down = jnp.sum(jnp.where(earlier == later, across, 0), axis=1, keepdims=True)
+    down = jnp.sum(jnp.where(earlier == later, across, 0.0), axis=1, keepdims=True)
     same = (across == down) & (earlier < later)
-    rank = jnp.sum(same.astype(jnp.int32), axis=0, keepdims=True)
+    rank = jnp.sum(same.astype(F32), axis=0, keepdims=True).astype(jnp.int32)
     return holder, rank
 
 
@@ -74,7 +74,8 @@
     local = panel_row - my_row() * rows_dev
     in_slot = place == iota((SLOTS, win), 0)
     mine = in_slot & (local >= 0) & (local < rows_dev)
-    source = jnp.sum(jnp.where(mine, local + 1, 0), axis=1, keepdims=True) - 1
+    spot = jnp.where(mine, (local + 1).astype(F32), 0.0)
+    source = jnp.sum(spot, axis=1, keepdims=True).astype(jnp.int32) - 1
     pick = (source == iota((SLOTS, rows_dev), 1)).astype(F32).astype(BF16)
     picked = contract(pick, border_ref[...], 1, 1)
     for z in range(z_count):
@@ -82,7 +83,8 @@
     share = win // lax.axis_size(SCEN)
     at = lax.axis_index(SCEN) * share + iota((share, win), 0)
     on_diagonal = at == iota((share, win), 1)
-    own = jnp.sum(jnp.where(on_diagonal, local, 0), axis=1, keepdims=True)
+    own = jnp.where(on_diagonal, local.astype(F32), 0.0)
+    own = jnp.sum(own, axis=1, keepdims=True).astype(jnp.int32)
     hit = own == iota((share, rows_dev), 1)
     first = first_ref[...]
     first_high = first.astype(BF16)

time: 129 us -> 129 us (level)
  no operation moved by 1% of the time
where the time goes in v10:
time: 129 us; the launch traced here: 128 us
  blocking collectives  89 us (69%)
  waiting for transfers between devices  13.7 us (11%)
  Pallas kernels  11.9 us (9%)
  starting transfers between devices  8.55 us (7%)
  local copies, waits for them, and re-layouts  2.17 us (2%)
    all_gather x1, blocking collectives, gather_round(): everyone = lax.all_gather(mine, 'z', axis=0)  36.5 us
    all_gather x1, blocking collectives, per_device(): gathered = lax.all_gather(message, 'z', axis=0)  24.2 us
    all_gather x1, blocking collectives, per_device(): given = lax.all_gather(give, 'core', axis=0)  17 us
    pallas_call x1, Pallas kernels, per_device(): pl.pallas_call(factor_kernel, out_shape=jax.ShapeDtypeStruct((rows_dev, w...  8.9 us
    all_to_all x1, waiting for transfers between devices, per_device(): shares = lax.all_to_all(pair, 'chip', 0, 0, tiled=True)  7.4 us
    all_gather x1, blocking collectives, gather_round(): both = lax.all_gather(message, 'xh', axis=0)  6.76 us
    all_to_all x1, waiting for transfers between devices, per_device(): everyone = lax.all_to_all(copies, 'chip', 0, 0, tiled=True)  6.28 us
    all_to_all x1, starting transfers between devices, per_device(): shares = lax.all_to_all(pair, 'chip', 0, 0, tiled=True)  5.12 us
  transfers between devices with their start and end apart: 2, of which 2 were waited for; matrix products, arithmetic and copies ran while one was open for 0% of the time, Pallas kernels for 0%

profile of v10, /device:TPU:1, one launch (start us, length us, event | category | flops | bytes accessed | tf_op | source)
XLA Modules:
  0.0 128.2 jit_solution(616201540455215313)
XLA Ops:
  0.7 0.0 copy-start.3
  0.7 0.0 copy-start.4
  0.7 0.7 copy-done.3
  1.3 0.0 copy-done.4
  1.4 2.2 %shard_map.73 = (bf16[71,1024]{1,0:T(8,128)(2,1)S(1)}, bf16[16,31,256]{2,1,0:T(8,128)(2,1)S(1)}, f32[1,256]{1,0:T(1,128)S(1)}, s32[1]{0:T(128)}) custom-call(s32[1]{0:T(128)} %constant.15.clone.1.turn_ref, f32[16]{0:T(128)S(1)} %copy-done.5, s32[1]{0:T(128)S(6)} %copy.14.slot_ref, s32[256]{0:T(256)S(1)} %copy-done.4, bf16[1024,384]{1,0:T(8,128)(2,1)} %bitcast.39, ...), custom_call_target="tpu_custom_call" | custom-call | tf_op jit(solution)/shard_map/pallas_call | solution.py:114
  3.5 6.8 %all-gather.6 = bf16[2,71,1024]{2,1,0:T(8,128)(2,1)S(1)} all-gather(bf16[1,71,1024]{2,1,0:T(8,128)(2,1)S(1)} %bitcast.38), channel_id=3, replica_groups=mesh['chip'=8,'core'=2,'z'=16,'xh'=2] {'xh'}, dimensions={0}, use_global_device_ids=true | all-gather | bytes 436224 | tf_op jit(solution)/shard_map/all_gather | solution.py:126
  10.3 36.5 %all_gather.40 = bf16[16,31,1024]{2,1,0:T(8,128)(2,1)S(1)} all-gather(bf16[1,31,1024]{2,1,0:T(8,128)(2,1)S(1)} %slice_add_fusion.1), channel_id=1, replica_groups=mesh['chip'=8,'core'=2,'z'=16,'xh'=2] {'z'}, dimensions={0}, use_global_device_ids=true | all-gather | bytes 1079296 | tf_op jit(solution)/shard_map/all_gather | solution.py:128
  46.8 0.5 fusion.2
  47.3 0.6 copy-done
  48.0 0.1 copy-done.1
  48.1 0.6 while.10
  48.7 0.2 shard_map.74
  48.9 24.2 %all-gather.2 = bf16[1536,256]{1,0:T(8,128)(2,1)S(1)} all-gather(bf16[96,256]{1,0:T(8,128)(2,1)S(1)} %shard_map.74), channel_id=4, replica_groups=mesh['chip'=8,'core'=2,'z'=16,'xh'=2] {'z'}, dimensions={0}, use_global_device_ids=true | all-gather | bytes 835584 | tf_op jit(solution)/shard_map/all_gather | solution.py:305
  73.2 0.6 shard_map.75
  73.8 17.0 %all-gather.3 = f32[16,40,256]{2,1,0:T(8,128)S(1)} all-gather(f32[8,40,256]{2,1,0:T(8,128)S(1)} %get-tuple-element.73), channel_id=5, replica_groups=mesh['chip'=8,'core'=2,'z'=16,'xh'=2] {'core'}, dimensions={0}, use_global_device_ids=true | all-gather | bytes 983040 | tf_op jit(solution)/shard_map/all_gather | solution.py:314
  90.8 0.8 bitcast_add_fusion
  91.6 5.1 %all-to-all-start = ((f32[8,40,256]{2,1,0:T(8,128)}), f32[8,40,256]{2,1,0:T(8,128)S(1)}, u32[]{:S(2)}, u32[]{:S(2)}) async-start(f32[8,40,256]{2,1,0:T(8,128)} %bitcast_add_fusion), calls=%async_computation | async-start | bytes 655360 | tf_op jit(solution)/shard_map/all_to_all | solution.py:316
  96.7 7.4 %all-to-all-done = f32[8,40,256]{2,1,0:T(8,128)S(1)} async-done(((f32[8,40,256]{2,1,0:T(8,128)}), f32[8,40,256]{2,1,0:T(8,128)S(1)}, u32[]{:S(2)}, u32[]{:S(2)}) %all-to-all-start) | async-done | bytes 327712 | tf_op jit(solution)/shard_map/all_to_all | solution.py:316
  104.1 0.7 broadcast_in_dim.24
  104.9 3.4 %all-to-all-start.1 = ((f32[8,40,256]{2,1,0:T(8,128)}), f32[8,40,256]{2,1,0:T(8,128)S(1)}, u32[]{:S(2)}, u32[]{:S(2)}) async-start(f32[8,40,256]{2,1,0:T(8,128)} %broadcast_in_dim.24), calls=%async_computation.1 | async-start | bytes 655360 | tf_op jit(solution)/shard_map/all_to_all | solution.py:319
  108.3 0.2 select_add_fusion.base_ref
  108.5 6.3 %all-to-all-done.1 = f32[8,40,256]{2,1,0:T(8,128)S(1)} async-done(((f32[8,40,256]{2,1,0:T(8,128)}), f32[8,40,256]{2,1,0:T(8,128)S(1)}, u32[]{:S(2)}, u32[]{:S(2)}) %all-to-all-start.1) | async-done | bytes 327712 | tf_op jit(solution)/shard_map/all_to_all | solution.py:319
  114.8 4.5 %all-gather.4 = f32[16,40,256]{2,1,0:T(8,128)S(1)} all-gather(f32[8,40,256]{2,1,0:T(8,128)S(1)} %all-to-all-done.1), channel_id=6, replica_groups=mesh['chip'=8,'core'=2,'z'=16,'xh'=2] {'core'}, dimensions={0}, use_global_device_ids=true | all-gather | bytes 983040 | tf_op jit(solution)/shard_map/all_gather | solution.py:320
  119.3 8.9 %shard_map.76 = f32[384,256]{1,0:T(8,128)} custom-call(f32[2,8,40,256]{3,2,1,0:T(8,128)S(1)} %bitcast.37, f32[384,256]{1,0:T(8,128)S(1)} %select_add_fusion.base_ref), custom_call_target="tpu_custom_call" | custom-call | tf_op jit(solution)/shard_map/pallas_call | solution.py:326
  (11 shorter events, 0.1 us)
Async XLA Ops:
  0.7 0.7 copy-start.3
  0.7 0.7 copy-start.4
  0.7 0.7 copy-start.5
  46.8 1.1 copy-start
  46.8 1.2 copy-start.1
  46.8 1.2 copy-start.2
  91.6 12.5 %all-to-all-start = ((f32[8,40,256]{2,1,0:T(8,128)}), f32[8,40,256]{2,1,0:T(8,128)S(1)}, u32[]{:S(2)}, u32[]{:S(2)}) async-start(f32[8,40,256]{2,1,0:T(8,128)} %bitcast_add_fusion), calls=%async_computation | async-start | bytes 655360 | tf_op jit(solution)/shard_map/all_to_all | solution.py:316
  104.9 9.9 %all-to-all-start.1 = ((f32[8,40,256]{2,1,0:T(8,128)}), f32[8,40,256]{2,1,0:T(8,128)S(1)}, u32[]{:S(2)}, u32[]{:S(2)}) async-start(f32[8,40,256]{2,1,0:T(8,128)} %broadcast_in_dim.24), calls=%async_computation.1 | async-start | bytes 655360 | tf_op jit(solution)/shard_map/all_to_all | solution.py:319
